TPU v7x, 256 devices: a whole 4x4x8 slice. The times are simulated.
256 devices in a mesh: row: 8 (over x, y_hi), col: 32 (over y_lo, z, core).
Axes of the slice: x: 4, y: 4 (y_hi: 2, y_lo: 2; y = y_hi * 2 + y_lo), z: 8, core: 2. Of those that a mesh axis runs over, the one named last changes fastest.
Arguments:
- pair_left: bfloat16 [1024, 256, 128], P('row', 'col'), may hold values from -6 to 6
- pair_right: bfloat16 [2048, 256, 128], P('col', 'row'), may hold values from -6 to 6
- pair_tile: bfloat16 [1024, 2048, 128], P('row', 'col'), may hold values from -6 to 6
- d_update: bfloat16 [1024, 2048, 128], P('row', 'col'), may hold values from -6 to 6
- mask_rows: int32 [1024], P('row'), may hold values 0 or 1
- mask_cols: int32 [2048], P('col'), may hold values 0 or 1
- mask_mid: int32 [256], replicated, may hold values 0 or 1
- ln_in_gain: float32 [128], replicated, may hold values from 0.1 to 1.9
- left_gate_w: bfloat16 [128, 128], replicated, may hold values from -0.5 to 0.5
- left_proj_w: bfloat16 [128, 128], replicated, may hold values from -0.5 to 0.5
- right_gate_w: bfloat16 [128, 128], replicated, may hold values from -0.5 to 0.5
- right_proj_w: bfloat16 [128, 128], replicated, may hold values from -0.5 to 0.5
- out_gate_w: bfloat16 [128, 128], replicated, may hold values from -0.5 to 0.5
- ln_mid_gain: float32 [128], replicated, may hold values from 0.1 to 1.9
- out_proj_w: bfloat16 [128, 128], replicated, may hold values from -0.5 to 0.5
Outputs:
- update: bfloat16 [1024, 2048, 128], P('row', 'col')
- d_pair_left: bfloat16 [1024, 256, 128], P('row', 'col')
- d_pair_right: bfloat16 [2048, 256, 128], P('col', 'row')
- d_pair_tile: bfloat16 [1024, 2048, 128], P('row', 'col')
All inputs are finite; a program needn't handle non-finite values. No bound on the sum of `mask_rows` or of `mask_cols` on one device may be relied on, other than what follows from the above.
Results may differ from a plain program's by a relative error of at most 0.03.
Values may be sent and summed in bfloat16 or wider, within the bound.
A program may use at most 128 MiB of HBM per device.

v0:
```python
import jax
import jax.numpy as jnp
from jax import lax
from jax.sharding import PartitionSpec as P


def layer_norm(values, gain):
    mean = jnp.mean(values, axis=-1, keepdims=True)
    centred = values - mean
    rstd = lax.rsqrt(jnp.mean(centred * centred, axis=-1, keepdims=True) + 1e-05)
    normed = centred * rstd
    return (normed * gain, normed, rstd)


def norm_back(normed, rstd, gain, upstream):
    scaled = upstream * gain
    inner = jnp.mean(scaled * normed, axis=-1, keepdims=True)
    return (scaled - jnp.mean(scaled, axis=-1, keepdims=True) - normed * inner) * rstd


def project_side(pair, mask_two, gain, gate_w, proj_w):
    normed_out, normed, rstd = layer_norm(pair.astype(jnp.float32), gain)
    rounded = normed_out.astype(jnp.bfloat16)
    gate = jax.nn.sigmoid(jnp.dot(rounded, gate_w, preferred_element_type=jnp.float32))
    value = jnp.dot(rounded, proj_w, preferred_element_type=jnp.float32)
    result = (mask_two[..., None] * gate * value).astype(jnp.bfloat16)
    return (result, gate, value, normed, rstd)


def side_back(grad, mask_two, gate, value, normed, rstd, gain, gate_w, proj_w):
    masked = grad * mask_two[..., None]
    d_value = (masked * gate).astype(jnp.bfloat16)
    d_gate = (masked * value * gate * (1.0 - gate)).astype(jnp.bfloat16)
    d_norm = jnp.dot(d_value, proj_w.T, preferred_element_type=jnp.float32)
    d_norm = d_norm + jnp.dot(d_gate, gate_w.T, preferred_element_type=jnp.float32)
    return norm_back(normed, rstd, gain, d_norm).astype(jnp.bfloat16)


def body(
    pair_left,
    pair_right,
    pair_tile,
    d_update,
    mask_rows,
    mask_cols,
    mask_mid,
    ln_in_gain,
    left_gate_w,
    left_proj_w,
    right_gate_w,
    right_proj_w,
    out_gate_w,
    ln_mid_gain,
    out_proj_w,
):
    mid_left = pair_left.shape[1]
    mid_right = pair_right.shape[1]
    midf = mask_mid.astype(jnp.float32)
    left_mid = lax.dynamic_slice_in_dim(midf, lax.axis_index("col") * mid_left, mid_left)
    right_mid = lax.dynamic_slice_in_dim(midf, lax.axis_index("row") * mid_right, mid_right)
    mask_left = mask_rows.astype(jnp.float32)[:, None] * left_mid[None, :]
    mask_right = mask_cols.astype(jnp.float32)[:, None] * right_mid[None, :]
    left, left_gate, left_value, left_normed, left_rstd = project_side(
        pair_left, mask_left, ln_in_gain, left_gate_w, left_proj_w
    )
    right, right_gate, right_value, right_normed, right_rstd = project_side(
        pair_right, mask_right, ln_in_gain, right_gate_w, right_proj_w
    )
    left_panel = lax.all_gather(left, "col", axis=1, tiled=True)
    right_panel = lax.all_gather(right, "row", axis=1, tiled=True)
    triangle = jnp.einsum(
        "ikc,jkc->ijc", left_panel, right_panel, preferred_element_type=jnp.float32
    )
    tri_out, tri_normed, tri_rstd = layer_norm(triangle, ln_mid_gain)
    tri_norm = tri_out.astype(jnp.bfloat16)
    tile_out, tile_normed, tile_rstd = layer_norm(pair_tile.astype(jnp.float32), ln_in_gain)
    tile_norm = tile_out.astype(jnp.bfloat16)
    out_gate = jax.nn.sigmoid(jnp.dot(tile_norm, out_gate_w, preferred_element_type=jnp.float32))
    out_value = jnp.dot(tri_norm, out_proj_w, preferred_element_type=jnp.float32)
    update = (out_gate * out_value).astype(jnp.bfloat16)
    upstream = d_update.astype(jnp.float32)
    d_value = (upstream * out_gate).astype(jnp.bfloat16)
    d_gate = (upstream * out_value * out_gate * (1.0 - out_gate)).astype(jnp.bfloat16)
    d_tri_norm = jnp.dot(d_value, out_proj_w.T, preferred_element_type=jnp.float32)
    d_tile_norm = jnp.dot(d_gate, out_gate_w.T, preferred_element_type=jnp.float32)
    d_triangle = norm_back(tri_normed, tri_rstd, ln_mid_gain, d_tri_norm).astype(jnp.bfloat16)
    d_pair_tile = norm_back(tile_normed, tile_rstd, ln_in_gain, d_tile_norm).astype(jnp.bfloat16)
    left_full = jnp.einsum(
        "ijc,jkc->kic", d_triangle, right_panel, preferred_element_type=jnp.float32
    )
    left_sum = lax.psum_scatter(
        left_full.astype(jnp.bfloat16), "col", scatter_dimension=0, tiled=True
    ).astype(jnp.float32)
    right_full = jnp.einsum(
        "ijc,ikc->kjc", d_triangle, left_panel, preferred_element_type=jnp.float32
    )
    right_sum = lax.psum_scatter(
        right_full.astype(jnp.bfloat16), "row", scatter_dimension=0, tiled=True
    ).astype(jnp.float32)
    d_left = jnp.swapaxes(left_sum, 0, 1)
    d_right = jnp.swapaxes(right_sum, 0, 1)
    d_pair_left = side_back(
        d_left,
        mask_left,
        left_gate,
        left_value,
        left_normed,
        left_rstd,
        ln_in_gain,
        left_gate_w,
        left_proj_w,
    )
    d_pair_right = side_back(
        d_right,
        mask_right,
        right_gate,
        right_value,
        right_normed,
        right_rstd,
        ln_in_gain,
        right_gate_w,
        right_proj_w,
    )
    return (update, d_pair_left, d_pair_right, d_pair_tile)


def solution(mesh):
    in_specs = (
        P("row", "col", None),
        P("col", "row", None),
        P("row", "col", None),
        P("row", "col", None),
        P("row"),
        P("col"),
        P(),
        P(),
        P(),
        P(),
        P(),
        P(),
        P(),
        P(),
        P(),
    )
    out_specs = (
        P("row", "col", None),
        P("row", "col", None),
        P("col", "row", None),
        P("row", "col", None),
    )
    return jax.shard_map(body, mesh=mesh, in_specs=in_specs, out_specs=out_specs, check_vma=False)
```

profile of v0, /device:TPU:1, one launch (start us, length us, event | category | flops | bytes accessed | tf_op | source)
XLA Modules:
  0.0 453.2 jit_solution(1467009413774181600)
XLA Ops:
  7.3 0.7 convert_element_type.88
  8.0 0.7 convert_element_type.89
  8.7 1.4 convert_reduce_fusion.1
  10.1 1.7 fusion.48
  11.7 0.1 dynamic_slice.6
  11.8 0.1 add_rsqrt_fusion.1
  11.9 2.0 fusion.32
  13.9 1.0 copy-done.5
  14.9 1.9 multiply_convert_fusion.3
  16.9 0.1 dynamic_slice.7
  17.0 0.2 copy.38
  17.3 0.1 fusion.65
  17.5 0.4 fusion.41
  17.9 1.2 multiply_convert_fusion.4
  19.2 3.3 copy.36
  22.5 0.5 convert_reduce_fusion
  23.0 0.8 fusion.10
  23.9 0.6 copy-done.12
  24.5 1.5 add_divide_fusion
  26.0 2.0 copy-done.1
  27.9 3.8 fusion.19
  31.7 71.5 %all-gather.3.cloned.1.call-done = bf16[64,256,128]{2,1,0:T(8,128)(2,1)} async-done(((bf16[64,32,128]{2,1,0:T(8,128)(2,1)}), bf16[64,256,128]{2,1,0:T(8,128)(2,1)}) %all-gather.3.cloned.1.call-update) | async-done | bytes 4194320 | tf_op jit(solution)/shard_map/all_gather | solution.py:70
  103.2 15.6 %copy.41 = bf16[64,256,128]{0,1,2:T(8,128)(2,1)} copy(bf16[64,256,128]{2,1,0:T(8,128)(2,1)} %all-gather.3.cloned.1.call-done) | data formatting | bytes 8388608 | tf_op jit(solution)/shard_map/all_gather | solution.py:70
  118.8 59.3 %all-gather.5.cloned.1.call-done = bf16[128,256,128]{2,0,1:T(8,128)(2,1)} async-done(((bf16[128,8,128]{2,0,1:T(8,128)(2,1)}), bf16[128,256,128]{2,0,1:T(8,128)(2,1)}) %all-gather.5.cloned.1.call-update) | async-done | bytes 8388624 | tf_op jit(solution)/shard_map/all_gather | solution.py:69
  178.1 11.8 %copy.42 = bf16[128,256,128]{0,1,2:T(8,128)(2,1)} copy(bf16[128,256,128]{2,0,1:T(8,128)(2,1)} %all-gather.5.cloned.1.call-done) | data formatting | bytes 16777216 | tf_op jit(solution)/shard_map/all_gather | solution.py:69
  189.9 8.8 %bitcast_reduce_fusion = (f32[128,64]{0,1:T(8,128)S(1)}, f32[128,64,128]{2,1,0:T(8,128)S(1)}) fusion(bf16[64,256,128]{0,1,2:T(8,128)(2,1)} %copy.41, bf16[128,256,128]{0,1,2:T(8,128)(2,1)} %copy.42), kind=kOutput, calls=%fused_computation.21 | convolution fusion | flops 537911296 | bytes 16809984 | tf_op jit(solution)/shard_map/ikc,jkc->ijc/dot_general | solution.py:71
  198.7 0.5 multiply_reduce_fusion.1
  199.2 1.7 copy-done.3
  200.9 3.0 fusion.16
  203.9 6.9 %multiply_convert_fusion = (bf16[128,64,128]{0,1,2:T(8,128)(2,1)}, bf16[128,64,128]{0,1,2:T(8,128)(2,1)}) fusion(f32[128,64,128]{2,1,0:T(8,128)S(1)} %get-tuple-element.27, f32[128,64,128]{0,2,1:T(8,128)S(1)} %copy-done.3, f32[128,64]{0,1:T(8,128)S(1)} %broadcast_multiply_fusion.6, f32[128,64]{0,1:T(8,128)S(1)} %broadcast_multiply_fusion.7, ...), kind=kLoop, calls=%fused_computation.24 | loop fusion | flops 10485760 | bytes 12714496 | tf_op jit(solution)/shard_map/convert_element_type | solution.py:86
  210.8 9.0 %fusion.108 = bf16[128,256,64]{1,2,0:T(8,128)(2,1)} fusion(bf16[128,256,128]{0,1,2:T(8,128)(2,1)} %copy.42, bf16[128,64,128]{0,1,2:T(8,128)(2,1)} %get-tuple-element.20), kind=kOutput, calls=%fused_computation.143 | convolution fusion | flops 536870912 | bytes 14680064 | tf_op jit(solution)/shard_map/ijc,ikc->kjc/dot_general | solution.py:94
  219.8 6.9 %copy.49 = bf16[128,256,64]{0,1,2:T(8,128)(2,1)} copy(bf16[128,256,64]{1,2,0:T(8,128)(2,1)} %fusion.108) | data formatting | bytes 8388608 | tf_op jit(solution)/shard_map/ijc,ikc->kjc/dot_general | solution.py:94
  226.7 9.5 %fusion.107 = bf16[128,256,128]{2,1,0:T(8,128)(2,1)} fusion(bf16[64,256,128]{0,1,2:T(8,128)(2,1)} %copy.41, bf16[128,64,128]{0,1,2:T(8,128)(2,1)} %get-tuple-element.20), kind=kOutput, calls=%fused_computation.142 | convolution fusion | flops 536870912 | bytes 14680064 | tf_op jit(solution)/shard_map/ijc,jkc->kic/dot_general | solution.py:88
  236.3 12.7 %copy.47 = bf16[128,256,128]{0,2,1:T(8,128)(2,1)} copy(bf16[128,256,128]{2,1,0:T(8,128)(2,1)} %fusion.107) | data formatting | bytes 16777216 | tf_op jit(solution)/shard_map/ijc,jkc->kic/dot_general | solution.py:88
  249.0 5.8 %multiply_convert_fusion.1 = (bf16[128,64,128]{2,0,1:T(8,128)(2,1)S(1)}, f32[128,64,128]{2,0,1:T(8,128)S(1)}) fusion(f32[128,64,128]{2,0,1:T(8,128)} %copy-done.1, bf16[128,128]{1,0:T(8,128)(2,1)S(1)} %copy-done, bf16[128,64,128]{0,1,2:T(8,128)(2,1)} %get-tuple-element.21), kind=kOutput, calls=%fused_computation.26 | convolution fusion | flops 270532608 | bytes 12615680 | tf_op jit(solution)/shard_map/dot_general | solution.py:79
  254.8 2.7 copy.50
  257.5 3.0 multiply_reduce_fusion.2
  260.5 2.8 fusion.9
  263.3 4.3 copy.52
  267.6 47.3 %reduce-scatter.5.cloned.1.call-done = bf16[32,64,128]{2,0,1:T(8,128)(2,1)} async-done(((bf16[256,64,128]{2,0,1:T(8,128)(2,1)}), bf16[32,64,128]{2,0,1:T(8,128)(2,1)}) %reduce-scatter.5.cloned.1.call-update) | async-done | bytes 524304 | tf_op jit(solution)/shard_map/reduce_scatter | solution.py:97
  314.9 1.5 fusion.67
  316.5 2.6 fusion.105
  319.1 1.9 fusion.47
  321.0 121.7 %reduce-scatter.3.cloned.1.call-done = bf16[8,128,128]{2,1,0:T(8,128)(2,1)} async-done(((bf16[256,128,128]{2,1,0:T(8,128)(2,1)}), bf16[8,128,128]{2,1,0:T(8,128)(2,1)}) %reduce-scatter.3.cloned.1.call-update) | async-done | bytes 262160 | tf_op jit(solution)/shard_map/reduce_scatter | solution.py:91
  442.7 1.3 fusion.82
  444.1 1.5 fusion.106
  445.6 0.1 fusion.64
  445.8 0.9 copy.51
  (67 shorter events, 0.5 us)
Async XLA Ops:
  7.2 20.8 %copy-start = (bf16[128,128]{1,0:T(8,128)(2,1)S(1)}, bf16[128,128]{1,0:T(8,128)(2,1)}, u32[]{:S(2)}) copy-start(bf16[128,128]{1,0:T(8,128)(2,1)} %param.29) | copy-start | bytes 98308
  7.2 7.7 %copy-start.4 = (bf16[64,32,128]{2,1,0:T(8,128)(2,1)S(1)}, bf16[64,32,128]{2,1,0:T(8,128)(2,1)}, u32[]{:S(2)}) copy-start(bf16[64,32,128]{2,1,0:T(8,128)(2,1)} %param.16) | copy-start | bytes 1572868
  7.2 7.7 %copy-start.20 = (f32[128]{0:T(128)S(1)}, f32[128]{0:T(128)}, u32[]{:S(2)}) copy-start(f32[128]{0:T(128)} %param.22) | copy-start | bytes 1540
  7.2 7.7 %copy-start.15 = (bf16[128,128]{1,0:T(8,128)(2,1)S(1)}, bf16[128,128]{1,0:T(8,128)(2,1)}, u32[]{:S(2)}) copy-start(bf16[128,128]{1,0:T(8,128)(2,1)} %param.26) | copy-start | bytes 98308
  7.2 96.0 %all-gather.3.cloned.1.call-start = ((), (), s32[]{:S(2)}) async-start(), calls=%async_computation.2 | async-start | bytes 4718592 | tf_op jit(solution)/shard_map/all_gather | solution.py:70
  11.9 5.0 %copy-start.22 = (s32[128]{0:T(128)S(1)}, s32[128]{0:T(128)}, u32[]{:S(2)}) copy-start(s32[128]{0:T(128)} %param.19) | copy-start | bytes 1540
  11.9 5.1 %copy-start.14 = (bf16[128,8,128]{2,1,0:T(8,128)(2,1)S(1)}, bf16[128,8,128]{2,1,0:T(8,128)(2,1)}, u32[]{:S(2)}) copy-start(bf16[128,8,128]{2,1,0:T(8,128)(2,1)} %param.15) | copy-start | bytes 786436
  11.9 5.6 %copy-start.19 = (bf16[128,128]{1,0:T(8,128)(2,1)S(1)}, bf16[128,128]{1,0:T(8,128)(2,1)}, u32[]{:S(2)}) copy-start(bf16[128,128]{1,0:T(8,128)(2,1)} %param.23) | copy-start | bytes 98308
  13.9 1.0 copy-start.5
  13.9 3.9 copy-start.16
  16.8 161.3 %all-gather.5.cloned.1.call-start = ((), (), s32[]{:S(2)}) async-start(), calls=%async_computation.3 | async-start | bytes 8650752 | tf_op jit(solution)/shard_map/all_gather | solution.py:69
  19.1 295.8 %reduce-scatter.5.cloned.1.call-start = ((), (), s32[]{:S(2)}) async-start(), calls=%async_computation.5 | async-start | bytes 4718592 | tf_op jit(solution)/shard_map/reduce_scatter | solution.py:97
  22.5 2.0 copy-start.17
  23.0 0.9 copy-start.10
  23.9 0.6 copy-start.12
  24.5 3.4 copy-start.7
  26.0 2.0 copy-start.1
  198.7 2.2 copy-start.3
  198.7 2.2 copy-start.21
  226.7 216.0 %reduce-scatter.3.cloned.1.call-start = ((), (), s32[]{:S(2)}) async-start(), calls=%async_computation.4 | async-start | bytes 8650752 | tf_op jit(solution)/shard_map/reduce_scatter | solution.py:91
  249.0 8.5 %copy-start.8 = (bf16[128,64,128]{2,1,0:T(8,128)(2,1)S(1)}, bf16[128,64,128]{2,1,0:T(8,128)(2,1)}, u32[]{:S(2)}) copy-start(bf16[128,64,128]{2,1,0:T(8,128)(2,1)} %param.18) | copy-start | bytes 6291460
  249.0 8.5 %copy-start.11 = (f32[128,64]{0,1:T(8,128)S(1)}, f32[128,64]{0,1:T(8,128)}, u32[]{:S(2)}) copy-start(f32[128,64]{0,1:T(8,128)} %copy-done.10) | copy-start | bytes 98308
  249.0 8.5 %copy-start.13 = (f32[128,64]{0,1:T(8,128)S(1)}, f32[128,64]{0,1:T(8,128)}, u32[]{:S(2)}) copy-start(f32[128,64]{0,1:T(8,128)} %copy-done.12) | copy-start | bytes 98308
  249.0 8.5 %copy-start.18 = (bf16[128,128]{1,0:T(8,128)(2,1)S(1)}, bf16[128,128]{1,0:T(8,128)(2,1)}, u32[]{:S(2)}) copy-start(bf16[128,128]{1,0:T(8,128)(2,1)} %param.27) | copy-start | bytes 98308
  254.8 2.7 copy-start.2
  263.3 51.6 %copy-start.6 = (f32[64,32,128]{2,1,0:T(8,128)S(1)}, f32[64,32,128]{2,1,0:T(8,128)}, u32[]{:S(2)}) copy-start(f32[64,32,128]{2,1,0:T(8,128)} %copy-done.5) | copy-start | bytes 3145732
  263.3 53.1 %copy-start.9 = (f32[64,32,128]{2,1,0:T(8,128)S(1)}, f32[64,32,128]{2,1,0:T(8,128)}, u32[]{:S(2)}) copy-start(f32[64,32,128]{2,1,0:T(8,128)} %get-tuple-element.23) | copy-start | bytes 3145732
Sparse Core Ops, SparseCore 0:
  17.0 86.1 all-gather.2
  105.6 72.4 all-gather.4
  226.8 88.0 reduce-scatter.4
  317.3 125.3 reduce-scatter.2
where the time goes:
time: 458 us; the launch traced here: 453 us
  waiting for transfers between devices  300 us (66%)
  local copies, waits for them, and re-layouts  63.9 us (14%)
  matrix products  53.7 us (12%)
  other arithmetic  21.4 us (5%)
  between operations  14.2 us (3%)
    reduce_scatter x1, waiting for transfers between devices, body(): lax.psum_scatter(left_full.astype(jnp.bfloat16), 'col', scatter_dimension...  122 us
    all_gather x1, waiting for transfers between devices, body(): right_panel = lax.all_gather(right, 'row', axis=1, tiled=True)  71.5 us
    all_gather x1, waiting for transfers between devices, body(): left_panel = lax.all_gather(left, 'col', axis=1, tiled=True)  59.3 us
    reduce_scatter x1, waiting for transfers between devices, body(): lax.psum_scatter(right_full.astype(jnp.bfloat16), 'row', scatter_dimensio...  47.3 us
    unnamed x51, local copies, waits for them, and re-layouts  16.7 us
    all_gather x1, local copies, waits for them, and re-layouts, body(): right_panel = lax.all_gather(right, 'row', axis=1, tiled=True)  15.6 us
    dot_general x1, local copies, waits for them, and re-layouts, body(): jnp.einsum('ijc,jkc->kic', d_triangle, right_panel, preferred_element_typ...  12.7 us
    all_gather x1, local copies, waits for them, and re-layouts, body(): left_panel = lax.all_gather(left, 'col', axis=1, tiled=True)  11.8 us
  transfers between devices with their start and end apart: 4, of which 4 were waited for; matrix products, arithmetic and copies ran while one was open for 16% of the time, Pallas kernels for 0%

commit v1 on v0

v1 whole, which is shorter than its diff:
```python
import functools

import jax
import jax.numpy as jnp
from jax import lax
from jax.experimental import pallas as pl
from jax.experimental.pallas import tpu as pltpu
from jax.sharding import PartitionSpec as P

MESH = pl.DeviceIdType.MESH
BF = jnp.bfloat16
F32 = jnp.float32
VMEM = pl.BlockSpec(memory_space=pltpu.VMEM)
SMEM = pl.BlockSpec(memory_space=pltpu.SMEM)
ANY = pl.BlockSpec(memory_space=pl.ANY)
LIMIT = 60 * 1024 * 1024


def nn(a, b):
    return lax.dot_general(a, b, (((1,), (0,)), ((), ())), preferred_element_type=F32)


def nt(a, b):
    return lax.dot_general(a, b, (((1,), (1,)), ((), ())), preferred_element_type=F32)


def tn(a, b):
    return lax.dot_general(a, b, (((0,), (0,)), ((), ())), preferred_element_type=F32)


def sigmoid(v):
    return 0.5 * jnp.tanh(0.5 * v) + 0.5


def norm(values, axis):
    centred = values - jnp.mean(values, axis=axis, keepdims=True)
    rstd = lax.rsqrt(jnp.mean(centred * centred, axis=axis, keepdims=True) + 1e-05)
    return centred * rstd, rstd


def norm_back(normed, rstd, gain, upstream, axis):
    scaled = upstream * gain
    inner = jnp.mean(scaled * normed, axis=axis, keepdims=True)
    return (scaled - jnp.mean(scaled, axis=axis, keepdims=True) - normed * inner) * rstd


def left_mask(mid_ref, rows_ref, k):
    keep = mid_ref[lax.axis_index("col") * 8 + k].astype(F32)
    return rows_ref[...].astype(F32) * keep


def right_mask(mid_ref, cols_ref, k):
    base = lax.axis_index("row") * 32 + k
    low = mid_ref[base].astype(F32)
    high = mid_ref[base + 16].astype(F32)
    lane = lax.broadcasted_iota(jnp.int32, (1, 128), 1)
    return cols_ref[...].astype(F32) * jnp.where(lane < 64, low, high)


def side_kernel(
    left_ref, right_ref, rows_ref, cols_ref, mid_ref, gain_ref, lg, lp, rg, rp,
    left_out, right_out, flat, wide,
):
    gain = gain_ref[...]

    def project(ref, count, weights):
        @pl.loop(0, count // 256)
        def _(t):
            rows = pl.ds(pl.multiple_of(t * 256, 256), 256)
            normed, _ = norm(ref[rows, :].astype(F32), -1)
            both = nn((normed * gain).astype(BF), weights)
            flat[rows, :] = sigmoid(both[:, :128]) * both[:, 128:]

    project(left_ref, 1024, jnp.concatenate([lg[...], lp[...]], axis=1))

    @pl.loop(0, 8)
    def _(k):
        turned = flat[pl.ds(k, 128, stride=8), :].T
        left_out[pl.ds(k, 128, stride=8), :] = turned * left_mask(mid_ref, rows_ref, k)

    project(right_ref, 2048, jnp.concatenate([rg[...], rp[...]], axis=1))

    @pl.loop(0, 16)
    def _(k):
        low = flat[pl.ds(k, 64, stride=32), :]
        high = flat[pl.ds(k + 16, 64, stride=32), :]
        turned = jnp.concatenate([low, high], axis=0).T
        wide[pl.ds(k, 128, stride=16), :] = turned * right_mask(mid_ref, cols_ref, k)

    @pl.loop(0, 8)
    def _(t):
        rows = pl.ds(pl.multiple_of(t * 256, 256), 256)
        right_out[rows, :] = wide[rows, :].astype(BF)


def side_back_kernel(
    left_ref, right_ref, dl_ref, dr_ref, rows_ref, cols_ref, mid_ref, gain_ref,
    lg, lp, rg, rp, left_out, right_out, flat,
):
    gain = gain_ref[...]

    def back(ref, count, gate_w, proj_w, out):
        weights = jnp.concatenate([gate_w[...], proj_w[...]], axis=1)

        @pl.loop(0, count // 256)
        def _(t):
            rows = pl.ds(pl.multiple_of(t * 256, 256), 256)
            normed, rstd = norm(ref[rows, :].astype(F32), -1)
            both = nn((normed * gain).astype(BF), weights)
            gate = sigmoid(both[:, :128])
            value = both[:, 128:]
            masked = flat[rows, :]
            d_value = (masked * gate).astype(BF)
            d_gate = (masked * value * gate * (1.0 - gate)).astype(BF)
            d_norm = nt(jnp.concatenate([d_gate, d_value], axis=1), weights)
            out[rows, :] = norm_back(normed, rstd, gain, d_norm, -1).astype(BF)

    @pl.loop(0, 8)
    def _(k):
        rows = dl_ref[pl.ds(k, 128, stride=8), :] * left_mask(mid_ref, rows_ref, k)
        flat[pl.ds(k, 128, stride=8), :] = rows.T

    back(left_ref, 1024, lg, lp, left_out)

    @pl.loop(0, 16)
    def _(k):
        rows = dr_ref[pl.ds(k, 128, stride=16), :] * right_mask(mid_ref, cols_ref, k)
        turned = rows.T
        flat[pl.ds(k, 64, stride=32), :] = turned[:64, :]
        flat[pl.ds(k + 16, 64, stride=32), :] = turned[64:, :]

    back(right_ref, 2048, rg, rp, right_out)


class Place:
    def __init__(self):
        row, col = lax.axis_index("row"), lax.axis_index("col")
        self.row, self.col = row, col
        self.x, self.yh = row // 2, lax.rem(row, 2)
        self.yl, self.z = col // 16, lax.rem(col // 2, 8)
        self.e = lax.rem(col, 2)

    def at(self, x=None, y=None, z=None, e=None):
        here = self.yh * 2 + self.yl
        y = here if y is None else lax.rem(here + y + 4, 4)
        x = self.x if x is None else lax.rem(self.x + x + 4, 4)
        z = self.z if z is None else lax.rem(self.z + z + 8, 8)
        e = self.e if e is None else 1 - self.e
        return (x * 2 + y // 2, lax.rem(y, 2) * 16 + z * 2 + e)

    def mate(self):
        return (self.row, (1 - self.yl) * 16 + self.z * 2 + self.e)

    def slot(self, same_y, dz):
        z = lax.rem(self.z + dz + 8, 8)
        yl = self.yl if same_y else 1 - self.yl
        return lax.rem(z, 2), yl * 4 + z // 2

    def across(self, same_y, dx):
        x = lax.rem(self.x + dx + 4, 4)
        yh = self.yh if same_y else 1 - self.yh
        return x * 2 + yh


def greet(place):
    barrier = pltpu.get_barrier_semaphore()
    partners = [
        place.at(e=1), place.at(z=1), place.at(z=-1), place.at(x=1), place.at(x=-1),
        place.at(y=1), place.at(y=-1),
    ]
    for partner in partners:
        pl.semaphore_signal(barrier, inc=1, device_id=partner, device_id_type=MESH)
    pl.semaphore_wait(barrier, len(partners))


class Wire:
    def __init__(self, send, recv):
        self.send, self.recv = send, recv
        self.number, self.open = {}, []

    def copy(self, name, src, dst, to):
        index = self.number.setdefault(name, len(self.number))
        return pltpu.make_async_remote_copy(
            src_ref=src, dst_ref=dst, send_sem=self.send.at[index],
            recv_sem=self.recv.at[index], device_id=to, device_id_type=MESH,
        )

    def start(self, name, src, dst, to):
        made = self.copy(name, src, dst, to)
        made.start()
        self.open.append(made)

    def arrived(self, name, dst, to):
        self.copy(name, dst, dst, to).wait_recv()

    def finish(self):
        for made in self.open:
            made.wait_send()


def gather_kernel(
    left_ref, right_ref, lp, rp, given, own, relay, send, recv, local
):
    me = Place()
    wire = Wire(send, recv)
    half = pl.ds(pl.multiple_of(me.e * 64, 64), 64)
    other = pl.ds(pl.multiple_of((1 - me.e) * 64, 64), 64)
    core, up, down = me.at(e=1), me.at(z=1), me.at(z=-1)
    east, west, north, south = me.at(x=1), me.at(x=-1), me.at(y=1), me.at(y=-1)
    low, high = pl.ds(0, 64), pl.ds(64, 64)
    greet(me)

    wire.start("core", left_ref.at[other], given, core)
    mine = rp.at[me.row]
    wire.start("ya", right_ref.at[low], relay.at[0], north)
    wire.start("yb", right_ref.at[high], relay.at[1], south)
    wire.start("x+a1", right_ref.at[low], mine.at[low], east)
    wire.start("x-b1", right_ref.at[high], mine.at[high], west)
    wire.start("x+b1", right_ref.at[high], mine.at[high], east)
    wire.start("x-a1", right_ref.at[low], mine.at[low], west)
    keep_right = pltpu.make_async_copy(right_ref, mine, local.at[0])
    keep_right.start()

    wire.arrived("core", given, core)

    @pl.loop(0, 8)
    def _(t):
        part = pl.ds(pl.multiple_of(t * 8, 8), 8)
        ours = left_ref[pl.ds(pl.multiple_of(me.e * 64 + t * 8, 8), 8)]
        theirs = given[part]
        first = jnp.where(me.e == 0, ours, theirs)
        second = jnp.where(me.e == 0, theirs, ours)
        own[part] = jnp.concatenate([first, second], axis=1).astype(BF)

    def piece(same_y, dz, part=half):
        kh, slot = me.slot(same_y, dz)
        return lp.at[kh, slot, part]

    def share(name, same_y, dz, src=None):
        ref = piece(same_y, dz)
        wire.start("c" + name, ref if src is None else src, ref, core)

    keep_left = pltpu.make_async_copy(own, piece(True, 0), local.at[1])
    wire.start("mate", own, piece(True, 0), me.mate())
    wire.start("z+O1", own, piece(True, 0), up)
    wire.start("z-O1", own, piece(True, 0), down)
    keep_left.start()
    share("O0", True, 0, own)

    def through_y():
        above, below = lax.rem(me.yh * 2 + me.yl + 3, 4), lax.rem(me.yh * 2 + me.yl + 1, 4)
        wire.arrived("ya", relay.at[0], north)
        wire.start("ya2", relay.at[0], rp.at[me.x * 2 + above // 2, low], north)
        wire.arrived("yb", relay.at[1], south)
        wire.start("yb2", relay.at[1], rp.at[me.x * 2 + below // 2, high], south)

    def left_step(src, d):
        same = src == "O"
        tag = src + str(d)
        later = src + str(d + 1)
        behind, ahead = piece(same, -d), piece(same, d)
        wire.arrived("z+" + tag, behind, up)
        wire.arrived("z-" + tag, ahead, down)
        if d < 3:
            wire.start("z+" + later, behind, behind, up)
            wire.start("z-" + later, ahead, ahead, down)
        else:
            front = pl.ds(pl.multiple_of(me.e * 64, 32), 32)
            rear = pl.ds(pl.multiple_of(me.e * 64 + 32, 32), 32)
            one, two = piece(same, -3, front), piece(same, 3, rear)
            wire.start("z+" + later, one, one, up)
            wire.start("z-" + later, two, two, down)
        share("+" + tag, same, -d)
        share("-" + tag, same, d)

    def left_last(src):
        same = src == "O"
        front = pl.ds(pl.multiple_of(me.e * 64, 32), 32)
        rear = pl.ds(pl.multiple_of(me.e * 64 + 32, 32), 32)
        wire.arrived("z+" + src + "4", piece(same, 4, front), up)
        wire.arrived("z-" + src + "4", piece(same, 4, rear), down)
        share("+" + src + "4", same, 4)

    def right_step(same, tag):
        west_ref, east_ref = rp.at[me.across(same, -1)], rp.at[me.across(same, 1)]
        wire.arrived("x+a" + tag + "1", west_ref.at[low], east)
        wire.start("x+a" + tag + "2", west_ref.at[low], west_ref.at[low], east)
        wire.arrived("x-b" + tag + "1", east_ref.at[high], west)
        wire.start("x-b" + tag + "2", east_ref.at[high], east_ref.at[high], west)

    def right_rest(same, tag):
        west_ref, east_ref = rp.at[me.across(same, -1)], rp.at[me.across(same, 1)]
        far = rp.at[me.across(same, 2)]
        wire.arrived("x+b" + tag + "1", west_ref.at[high], east)
        wire.arrived("x-a" + tag + "1", east_ref.at[low], west)
        wire.arrived("x+a" + tag + "2", far.at[low], east)
        wire.arrived("x-b" + tag + "2", far.at[high], west)

    wire.arrived("mate", piece(False, 0), me.mate())
    wire.start("z+Y1", piece(False, 0), piece(False, 0), up)
    wire.start("z-Y1", piece(False, 0), piece(False, 0), down)
    share("Y0", False, 0)
    wire.arrived("x+a1", rp.at[me.across(True, -1), low], east)
    wire.start("x+a2", rp.at[me.across(True, -1), low], rp.at[me.across(True, -1), low], east)
    wire.arrived("x-b1", rp.at[me.across(True, 1), high], west)
    wire.start("x-b2", rp.at[me.across(True, 1), high], rp.at[me.across(True, 1), high], west)
    through_y()
    left_step("O", 1)
    left_step("Y", 1)
    pair = rp.at[me.across(False, 0)]
    wire.arrived("ya2", pair.at[low], north)
    wire.start("x+ap1", pair.at[low], pair.at[low], east)
    wire.arrived("yb2", pair.at[high], south)
    wire.start("x-bp1", pair.at[high], pair.at[high], west)
    wire.start("x+bp1", pair.at[high], pair.at[high], east)
    wire.start("x-ap1", pair.at[low], pair.at[low], west)
    left_step("O", 2)
    left_step("Y", 2)
    right_step(False, "p")
    left_step("O", 3)
    left_step("Y", 3)
    right_rest(True, "")
    left_last("O")
    left_last("Y")
    right_rest(False, "p")
    for src in ("O", "Y"):
        same = src == "O"
        wire.arrived("c" + src + "0", piece(same, 0, other), core)
        for d in (1, 2, 3):
            wire.arrived("c+" + src + str(d), piece(same, -d, other), core)
            wire.arrived("c-" + src + str(d), piece(same, d, other), core)
        wire.arrived("c+" + src + "4", piece(same, 4, other), core)
    keep_right.wait()
    keep_left.wait()
    wire.finish()


def gather(left, right):
    return pl.pallas_call(
        gather_kernel,
        out_shape=(
            jax.ShapeDtypeStruct((2, 8, 128, 16, 128), BF),
            jax.ShapeDtypeStruct((8, 128, 16, 128), BF),
        ),
        in_specs=[VMEM, VMEM],
        out_specs=(ANY, ANY),
        scratch_shapes=[
            pltpu.VMEM((64, 8, 128), F32),
            pltpu.VMEM((64, 16, 128), BF),
            pltpu.VMEM((2, 64, 16, 128), BF),
            pltpu.SemaphoreType.DMA((56,)),
            pltpu.SemaphoreType.DMA((56,)),
            pltpu.SemaphoreType.DMA((2,)),
        ],
        compiler_params=pltpu.CompilerParams(
            collective_id=0, has_side_effects=True, vmem_limit_bytes=LIMIT
        ),
        name="gather_panels",
    )(left, right)


def scatter_kernel(
    dl, dr, left_out, right_out,
    ls, core_in, z_in, mate_in, give, got, rs, x_in, relay, pair_in,
    send, recv, local,
):
    me = Place()
    wire = Wire(send, recv)
    half = pl.ds(pl.multiple_of(me.e * 64, 64), 64)
    other = pl.ds(pl.multiple_of((1 - me.e) * 64, 64), 64)
    core, up, down = me.at(e=1), me.at(z=1), me.at(z=-1)
    east, west, north, south = me.at(x=1), me.at(x=-1), me.at(y=1), me.at(y=-1)
    low, high = pl.ds(0, 64), pl.ds(64, 64)
    greet(me)

    loads = {}
    for count, dz in enumerate((4, 3, 5, 2, 6, 1, 7, 0)):
        for which in (0, 1):
            kh, slot = me.slot(which == 1, dz)
            wire.start(
                f"c{which}{dz}", dl.at[kh, slot, other], core_in.at[which, dz], core
            )
            load = pltpu.make_async_copy(
                dl.at[kh, slot, half], ls.at[which, dz], local.at[which * 8 + dz]
            )
            load.start()
            loads[which, dz] = load
        if count < 4:
            dx = (2, 1, 3, 0)[count]
            for which in (0, 1):
                load = pltpu.make_async_copy(
                    dr.at[me.across(which == 1, dx)], rs.at[which, dx],
                    local.at[16 + which * 4 + dx],
                )
                load.start()
                loads["r", which, dx] = load

    def add(target, terms, count, start=0, out=None):
        @pl.loop(start // 8, (start + count) // 8)
        def _(t):
            part = pl.ds(pl.multiple_of(t * 8, 8), 8)
            total = target[part].astype(F32)
            for term in terms:
                total = total + term[part].astype(F32)
            if out is None:
                target[part] = total.astype(BF)
            else:
                out(part, total)

    def combine(which, dz):
        loads[which, dz].wait()
        wire.arrived(f"c{which}{dz}", core_in.at[which, dz], core)

    def left_first(which):
        combine(which, 4)
        block = ls.at[which, 4]
        add(block, [core_in.at[which, 4]], 64)
        front, rear = pl.ds(0, 32), pl.ds(32, 32)
        wire.start(f"z+{which}0", block.at[front], z_in.at[0, which, 0, front], up)
        wire.start(f"z-{which}0", block.at[rear], z_in.at[1, which, 0, rear], down)

    def left_step(which, d):
        for way, sign, to, dz in ((0, "+", up, 4 - d), (1, "-", down, 4 + d)):
            combine(which, dz)
            block, given = ls.at[which, dz], core_in.at[which, dz]
            came = z_in.at[way, which, d - 1]
            if d == 1:
                part = pl.ds(way * 32, 32)
                wire.arrived(f"z{sign}{which}0", came.at[part], to)
                add(block, [given, came], 32, way * 32)
                add(block, [given], 32, 32 - way * 32)
            else:
                wire.arrived(f"z{sign}{which}{d - 1}", came, to)
                add(block, [given, came], 64)
            wire.start(f"z{sign}{which}{d}", block, z_in.at[way, which, d], to)

    def left_last(which):
        combine(which, 0)
        wire.arrived(f"z+{which}3", z_in.at[0, which, 3], up)
        wire.arrived(f"z-{which}3", z_in.at[1, which, 3], down)
        return [core_in.at[which, 0], z_in.at[0, which, 3], z_in.at[1, which, 3]]

    def right_first(which):
        loads["r", which, 2].wait()
        block = rs.at[which, 2]
        wire.start(f"x+{which}0", block.at[low], x_in.at[0, which, 0, low], east)
        wire.start(f"x-{which}0", block.at[high], x_in.at[1, which, 0, high], west)

    def right_step(which):
        for way, sign, to, dx, part in (
            (0, "+", east, 1, low), (1, "-", west, 3, high),
        ):
            loads["r", which, dx].wait()
            came, block = x_in.at[way, which, 0], rs.at[which, dx]
            wire.arrived(f"x{sign}{which}0", came.at[part], to)
            add(block, [came], 64, way * 64)
            wire.start(f"x{sign}{which}1", block, x_in.at[way, which, 1], to)

    def right_last(which):
        loads["r", which, 0].wait()
        wire.arrived(f"x+{which}1", x_in.at[0, which, 1], east)
        wire.arrived(f"x-{which}1", x_in.at[1, which, 1], west)
        return [x_in.at[0, which, 1], x_in.at[1, which, 1]]

    left_first(0)
    right_first(0)
    left_first(1)
    right_first(1)
    left_step(0, 1)
    left_step(1, 1)
    right_step(0)
    right_step(1)
    left_step(0, 2)
    left_step(1, 2)
    left_step(0, 3)
    add(rs.at[0, 0], right_last(0), 128)
    wire.start("ya", rs.at[0, 0, low], relay.at[0], north)
    wire.start("yb", rs.at[0, 0, high], relay.at[1], south)
    left_step(1, 3)
    wire.arrived("ya", relay.at[0], north)
    wire.start("ya2", relay.at[0], pair_in.at[low], north)
    wire.arrived("yb", relay.at[1], south)
    wire.start("yb2", relay.at[1], pair_in.at[high], south)
    add(ls.at[0, 0], left_last(0), 64)
    wire.start("mate", ls.at[0, 0], mate_in, me.mate())
    terms = right_last(1)
    wire.arrived("ya2", pair_in.at[low], north)
    wire.arrived("yb2", pair_in.at[high], south)

    def put_right(part, total):
        right_out[part] = total

    add(rs.at[1, 0], terms + [pair_in], 128, out=put_right)
    terms = left_last(1)
    wire.arrived("mate", mate_in, me.mate())

    def put_left(part, total):
        first, second = total[:, :8], total[:, 8:]
        left_out[pl.ds(pl.multiple_of(me.e * 64 + part.start, 8), 8)] = jnp.where(
            me.e == 0, first, second
        )
        give[part] = jnp.where(me.e == 0, second, first)

    add(ls.at[1, 0], terms + [mate_in], 64, out=put_left)
    wire.start("last", give, got, core)
    wire.arrived("last", got, core)

    @pl.loop(0, 8)
    def _(t):
        part = pl.ds(pl.multiple_of(t * 8, 8), 8)
        left_out[pl.ds(pl.multiple_of((1 - me.e) * 64 + t * 8, 8), 8)] = got[part]

    wire.finish()


def scatter(dl, dr):
    return pl.pallas_call(
        scatter_kernel,
        out_shape=(
            jax.ShapeDtypeStruct((128, 8, 128), F32),
            jax.ShapeDtypeStruct((128, 16, 128), F32),
        ),
        in_specs=[ANY, ANY],
        out_specs=(VMEM, VMEM),
        scratch_shapes=[
            pltpu.VMEM((2, 8, 64, 16, 128), BF),
            pltpu.VMEM((2, 8, 64, 16, 128), BF),
            pltpu.VMEM((2, 2, 4, 64, 16, 128), BF),
            pltpu.VMEM((64, 16, 128), BF),
            pltpu.VMEM((64, 8, 128), F32),
            pltpu.VMEM((64, 8, 128), F32),
            pltpu.VMEM((2, 4, 128, 16, 128), BF),
            pltpu.VMEM((2, 2, 2, 128, 16, 128), BF),
            pltpu.VMEM((2, 64, 16, 128), BF),
            pltpu.VMEM((128, 16, 128), BF),
            pltpu.SemaphoreType.DMA((56,)),
            pltpu.SemaphoreType.DMA((56,)),
            pltpu.SemaphoreType.DMA((24,)),
        ],
        compiler_params=pltpu.CompilerParams(
            collective_id=1, has_side_effects=True, vmem_limit_bytes=LIMIT
        ),
        name="scatter_sums",
    )(dl, dr)


CS = 16
NC = 128 // CS
JS = 8
NJ = 64 // JS


def middle_kernel(
    lp, rp, tile_ref, up_ref, in_gain_ref, gate_w_ref, mid_gain_ref, proj_w_ref,
    update_ref, d_tile_ref, dl_ref, dr_ref, tri, flat,
):
    step = pl.program_id(0)

    @pl.when(step < NC)
    def _():
        for c in range(CS):
            right = rp[:, c].reshape(128, 128)
            turned = right.T
            sides = jnp.concatenate([turned[:64], turned[64:]], axis=1)
            left = jnp.concatenate(
                [lp[0, :, c].reshape(128, 128), lp[1, :, c].reshape(128, 128)], axis=0
            )
            result = nn(sides, left)
            rows = pl.ds(pl.multiple_of((step * CS + c) * 8, 8), 8)
            for block in range(NJ):
                tri[block, rows, :] = result[block * 8:(block + 1) * 8]

    @pl.when((step >= NC) & (step < NC + NJ))
    def _():
        block = tri.at[step - NC]
        mid_gain = mid_gain_ref[...]
        in_gain = in_gain_ref[...]
        proj_w = proj_w_ref[...]
        gate_w = gate_w_ref[...]

        for j in range(JS):
            normed, _ = norm(block[pl.ds(j, 128, stride=8), :], 0)
            value = tn((normed * mid_gain).astype(BF), proj_w)
            flat[pl.ds(j, 128, stride=8), :] = value

        for t in range(8):
            rows = pl.ds(t * 128, 128)
            items = pl.ds(t * 16, 16)
            tile = tile_ref[items].astype(F32).reshape(128, 128)
            upstream = up_ref[items].astype(F32).reshape(128, 128)
            normed, rstd = norm(tile, -1)
            gate = sigmoid(nn((normed * in_gain).astype(BF), gate_w))
            value = flat[rows, :]
            update_ref[items] = (gate * value).reshape(16, 8, 128).astype(BF)
            gated = upstream * gate
            flat[rows, :] = gated
            d_gate = (gated * value * (1.0 - gate)).astype(BF)
            d_norm = nt(d_gate, gate_w)
            d_tile = norm_back(normed, rstd, in_gain, d_norm, -1)
            d_tile_ref[items] = d_tile.reshape(16, 8, 128).astype(BF)

        for j in range(JS):
            here = pl.ds(j, 128, stride=8)
            normed, rstd = norm(block[here, :], 0)
            d_norm = nt(proj_w, flat[here, :].astype(BF))
            block[here, :] = norm_back(normed, rstd, mid_gain, d_norm, 0)

    @pl.when(step >= NC + NJ)
    def _():
        for c in range(CS):
            rows = pl.ds(pl.multiple_of(((step - NC - NJ) * CS + c) * 8, 8), 8)
            grad = jnp.concatenate(
                [tri[block, rows, :] for block in range(NJ)], axis=0
            ).astype(BF)
            none = jnp.zeros((64, 128), BF)
            grad = jnp.concatenate(
                [
                    jnp.concatenate([grad, none], axis=1),
                    jnp.concatenate([none, grad], axis=1),
                ],
                axis=0,
            )
            right = rp[:, c].reshape(128, 128)
            left = jnp.concatenate(
                [lp[0, :, c].reshape(128, 128), lp[1, :, c].reshape(128, 128)], axis=1
            )
            d_left = nn(right, grad).astype(BF)
            dl_ref[0, :, c] = d_left[:, :128].reshape(8, 16, 128)
            dl_ref[1, :, c] = d_left[:, 128:].reshape(8, 16, 128)
            dr_ref[:, c] = nt(left, grad).astype(BF).reshape(8, 16, 128)


def middle(lp, rp, tile, upstream, in_gain, gate_w, mid_gain, proj_w):
    def channel(s):
        return jnp.where(s < NC + NJ, jnp.minimum(s, NC - 1), s - NC - NJ)

    def column(s):
        return jnp.clip(s - NC, 0, NJ - 1)

    def later(s):
        return jnp.maximum(s - NC - NJ, 0)

    left = lambda at: pl.BlockSpec((2, 8, CS, 16, 128), lambda s: (0, 0, at(s), 0, 0))
    right = lambda at: pl.BlockSpec((8, CS, 16, 128), lambda s: (0, at(s), 0, 0))
    cell = pl.BlockSpec((128, JS, 128), lambda s: (0, column(s), 0))
    whole = pl.BlockSpec((128, 128), lambda s: (0, 0))
    line = pl.BlockSpec((1, 128), lambda s: (0, 0))
    return pl.pallas_call(
        middle_kernel,
        grid=(NC + NJ + NC,),
        out_shape=(
            jax.ShapeDtypeStruct((128, 64, 128), BF),
            jax.ShapeDtypeStruct((128, 64, 128), BF),
            jax.ShapeDtypeStruct((2, 8, 128, 16, 128), BF),
            jax.ShapeDtypeStruct((8, 128, 16, 128), BF),
        ),
        in_specs=[left(channel), right(channel), cell, cell, line, whole, whole, whole],
        out_specs=(cell, cell, left(later), right(later)),
        scratch_shapes=[
            pltpu.VMEM((NJ, 1024, 128), F32),
            pltpu.VMEM((1024, 128), F32),
        ],
        compiler_params=pltpu.CompilerParams(
            vmem_limit_bytes=LIMIT, dimension_semantics=("arbitrary",)
        ),
        name="middle",
    )(lp, rp, tile, upstream, in_gain, gate_w, mid_gain, proj_w)


def body(
    pair_left,
    pair_right,
    pair_tile,
    d_update,
    mask_rows,
    mask_cols,
    mask_mid,
    ln_in_gain,
    left_gate_w,
    left_proj_w,
    right_gate_w,
    right_proj_w,
    out_gate_w,
    ln_mid_gain,
    out_proj_w,
):
    flat_left = pair_left.reshape(1024, 128)
    flat_right = pair_right.reshape(2048, 128)
    rows = mask_rows.reshape(1, 128)
    cols = jnp.concatenate([mask_cols, mask_cols]).reshape(1, 128)
    gain = ln_in_gain.reshape(1, 128)
    weights = (left_gate_w, left_proj_w, right_gate_w, right_proj_w)
    left, right = pl.pallas_call(
        side_kernel,
        out_shape=(
            jax.ShapeDtypeStruct((1024, 128), F32),
            jax.ShapeDtypeStruct((2048, 128), BF),
        ),
        in_specs=[VMEM] * 4 + [SMEM] + [VMEM] * 5,
        out_specs=(VMEM, VMEM),
        scratch_shapes=[pltpu.VMEM((2048, 128), F32), pltpu.VMEM((2048, 128), F32)],
        compiler_params=pltpu.CompilerParams(vmem_limit_bytes=LIMIT),
        name="sides",
    )(flat_left, flat_right, rows, cols, mask_mid, gain, *weights)
    lp, rp = gather(left.reshape(128, 8, 128), right.reshape(128, 16, 128))
    mid_gain = jnp.broadcast_to(ln_mid_gain[:, None], (128, 128))
    update, d_tile, dl, dr = middle(
        lp, rp, pair_tile, d_update, gain, out_gate_w, mid_gain, out_proj_w
    )
    dl, dr = scatter(dl, dr)
    d_left, d_right = pl.pallas_call(
        side_back_kernel,
        out_shape=(
            jax.ShapeDtypeStruct((1024, 128), BF),
            jax.ShapeDtypeStruct((2048, 128), BF),
        ),
        in_specs=[VMEM] * 6 + [SMEM] + [VMEM] * 5,
        out_specs=(VMEM, VMEM),
        scratch_shapes=[pltpu.VMEM((2048, 128), F32)],
        compiler_params=pltpu.CompilerParams(vmem_limit_bytes=LIMIT),
        name="sides_back",
    )(
        flat_left, flat_right, dl.reshape(1024, 128), dr.reshape(2048, 128),
        rows, cols, mask_mid, gain, *weights,
    )
    return (
        update,
        d_left.reshape(128, 8, 128),
        d_right.reshape(64, 32, 128),
        d_tile,
    )


def solution(mesh):
    in_specs = (
        P("row", "col", None),
        P("col", "row", None),
        P("row", "col", None),
        P("row", "col", None),
        P("row"),
        P("col"),
        P(),
        P(),
        P(),
        P(),
        P(),
        P(),
        P(),
        P(),
        P(),
    )
    out_specs = (
        P("row", "col", None),
        P("row", "col", None),
        P("col", "row", None),
        P("row", "col", None),
    )
    return jax.shard_map(body, mesh=mesh, in_specs=in_specs, out_specs=out_specs, check_vma=False)
```

time: 458 us -> 176 us (0.38)
  waiting for transfers between devices: 300 us -> 0 us
  Pallas kernels: 0 us -> 172 us
  local copies, waits for them, and re-layouts: 63.9 us -> 1.37 us
  matrix products: 53.7 us -> 0 us
  other arithmetic: 21.4 us -> 1.28 us
  between operations: 14.2 us -> 0.65 us
    pallas_call x0 -> x5, Pallas kernels: none -> 172 us  [the longest x1 61.4 us: gather(): pl.pallas_call(gather_kernel, out_shape=(jax.ShapeDtypeStruct((2, 8, 128,...]
    reduce_scatter x2 -> x0, waiting for transfers between devices: 169 us -> none  [the longest x1 122 us: body(): lax.psum_scatter(left_full.astype(jnp.bfloat16), 'col', scatter_dimension...]
    all_gather x2 -> x0, waiting for transfers between devices: 131 us -> none  [the longest x1 71.5 us: body(): right_panel = lax.all_gather(right, 'row', axis=1, tiled=True)]
    dot_general x15 -> x0, matrix products: 53.7 us -> none  [the longest x1 9.52 us: body(): jnp.einsum('ijc,jkc->kic', d_triangle, right_panel, preferred_element_typ...]
    all_gather x2 -> x0, local copies, waits for them, and re-layouts: 27.4 us -> none  [the longest x1 15.6 us: body(): right_panel = lax.all_gather(right, 'row', axis=1, tiled=True)]
    dot_general x2 -> x0, local copies, waits for them, and re-layouts: 19.6 us -> none  [the longest x1 12.7 us: body(): jnp.einsum('ijc,jkc->kic', d_triangle, right_panel, preferred_element_typ...]
    unnamed x51 -> x0, local copies, waits for them, and re-layouts: 16.7 us -> none
    convert_element_type x7 -> x0, other arithmetic: 13.2 us -> none  [the longest x1 6.94 us: body(): norm_back(tri_normed, tri_rstd, ln_mid_gain, d_tri_norm)]
  transfers between devices with their start and end apart: 4 -> 0, of which waited for: 4 -> 0; matrix products, arithmetic and copies ran while one was open for 16% -> 0% of each run, Pallas kernels for 0% -> 0%
where the time goes in v1:
time: 176 us; the launch traced here: 175 us
  Pallas kernels  172 us (98%)
    pallas_call x1, Pallas kernels, gather(): pl.pallas_call(gather_kernel, out_shape=(jax.ShapeDtypeStruct((2, 8, 128,...  61.4 us
    pallas_call x1, Pallas kernels, scatter(): pl.pallas_call(scatter_kernel, out_shape=(jax.ShapeDtypeStruct((128, 8, 1...  53.6 us
    pallas_call x1, Pallas kernels, middle(): pl.pallas_call(middle_kernel, grid=(NC + NJ + NC,), out_shape=(jax.ShapeD...  35.1 us
    pallas_call x1, Pallas kernels, body(): pl.pallas_call(side_back_kernel, out_shape=(jax.ShapeDtypeStruct((1024, 1...  13 us
    pallas_call x1, Pallas kernels, body(): pl.pallas_call(side_kernel, out_shape=(jax.ShapeDtypeStruct((1024, 128),...  9.14 us

profile of v1, /device:TPU:1, one launch (start us, length us, event | category | flops | bytes accessed | tf_op | source)
XLA Modules:
  0.0 175.4 jit_solution(17299923967299402003)
XLA Ops:
  0.6 1.3 add_bitcast_fusion.cols_ref
  1.9 1.4 broadcast_in_dim.2.mid_gain_ref
  3.3 9.1 %sides.1 = (f32[1024,128]{1,0:T(8,128)}, bf16[2048,128]{1,0:T(8,128)(2,1)}) custom-call(bf16[1024,128]{1,0:T(8,128)(2,1)} %bitcast.14, bf16[2048,128]{1,0:T(8,128)(2,1)} %bitcast.12, s32[1,128]{1,0:T(1,128)} %bitcast.23, s32[1,128]{1,0:T(1,128)} %add_bitcast_fusion.cols_ref, s32[256]{0:T(256)} %mid_ref.3, f32[1,128]{1,0:T(1,128)} %bitcast.20, ...), custom_call_target="tpu_custom_call" | custom-call | tf_op jit(solution)/shard_map/sides/pallas_call | solution.py:693
  12.4 61.4 %gather_panels.1 = (bf16[2,8,128,16,128]{4,3,2,1,0:T(8,128)(2,1)}, bf16[8,128,16,128]{3,2,1,0:T(8,128)(2,1)}) custom-call(f32[128,8,128]{2,1,0:T(8,128)} %bitcast.17, bf16[128,16,128]{2,1,0:T(8,128)(2,1)} %bitcast.18), custom_call_target="tpu_custom_call" | custom-call | tf_op jit(solution)/shard_map/gather_panels/pallas_call | solution.py:339
  73.8 35.1 %middle.1 = (bf16[128,64,128]{2,1,0:T(8,128)(2,1)}, bf16[128,64,128]{2,1,0:T(8,128)(2,1)}, bf16[2,8,128,16,128]{4,3,2,1,0:T(8,128)(2,1)}, bf16[8,128,16,128]{3,2,1,0:T(8,128)(2,1)}) custom-call(bf16[2,8,128,16,128]{4,3,2,1,0:T(8,128)(2,1)} %get-tuple-element.18.lp, bf16[8,128,16,128]{3,2,1,0:T(8,128)(2,1)} %get-tuple-element.19.rp, ...), custom_call_target="tpu_custom_call" | custom-call | tf_op jit(solution)/shard_map/middle/pallas_call | solution.py:648
  108.9 53.6 %scatter_sums.1 = (f32[128,8,128]{2,1,0:T(8,128)}, f32[128,16,128]{2,1,0:T(8,128)}) custom-call(bf16[2,8,128,16,128]{4,3,2,1,0:T(8,128)(2,1)} %get-tuple-element.21.dl, bf16[8,128,16,128]{3,2,1,0:T(8,128)(2,1)} %get-tuple-element.22.dr), custom_call_target="tpu_custom_call" | custom-call | tf_op jit(solution)/shard_map/scatter_sums/pallas_call | solution.py:517
  162.5 13.0 %sides_back.1 = (bf16[1024,128]{1,0:T(8,128)(2,1)}, bf16[2048,128]{1,0:T(8,128)(2,1)}) custom-call(bf16[1024,128]{1,0:T(8,128)(2,1)} %bitcast.15, bf16[2048,128]{1,0:T(8,128)(2,1)} %bitcast.13, f32[1024,128]{1,0:T(8,128)} %bitcast.19, f32[2048,128]{1,0:T(8,128)} %bitcast.16, s32[1,128]{1,0:T(1,128)} %bitcast.24, s32[1,128]{1,0:T(1,128)} %add_bitcast_fusion.cols_ref, ...), custom_call_target="tpu_custom_call" | custom-call | tf_op jit(solution)/shard_map/sides_back/pallas_call | solution.py:711

commit v2 on v1

v2 whole, which is shorter than its diff:
```python
import functools

import jax
import jax.numpy as jnp
from jax import lax
from jax.experimental import pallas as pl
from jax.experimental.pallas import tpu as pltpu
from jax.sharding import PartitionSpec as P

MESH = pl.DeviceIdType.MESH
BF = jnp.bfloat16
F32 = jnp.float32
VMEM = pl.BlockSpec(memory_space=pltpu.VMEM)
SMEM = pl.BlockSpec(memory_space=pltpu.SMEM)
ANY = pl.BlockSpec(memory_space=pl.ANY)
LIMIT = 60 * 1024 * 1024


def nn(a, b):
    return lax.dot_general(a, b, (((1,), (0,)), ((), ())), preferred_element_type=F32)


def nt(a, b):
    return lax.dot_general(a, b, (((1,), (1,)), ((), ())), preferred_element_type=F32)


def tn(a, b):
    return lax.dot_general(a, b, (((0,), (0,)), ((), ())), preferred_element_type=F32)


def sigmoid(v):
    return 0.5 * jnp.tanh(0.5 * v) + 0.5


def norm(values, axis):
    centred = values - jnp.mean(values, axis=axis, keepdims=True)
    rstd = lax.rsqrt(jnp.mean(centred * centred, axis=axis, keepdims=True) + 1e-05)
    return centred * rstd, rstd


def norm_back(normed, rstd, gain, upstream, axis):
    scaled = upstream * gain
    inner = jnp.mean(scaled * normed, axis=axis, keepdims=True)
    return (scaled - jnp.mean(scaled, axis=axis, keepdims=True) - normed * inner) * rstd


def left_mask(mid_ref, rows_ref, k):
    keep = mid_ref[lax.axis_index("col") * 8 + k].astype(F32)
    return rows_ref[...].astype(F32) * keep


def right_mask(mid_ref, cols_ref, k):
    base = lax.axis_index("row") * 32 + k
    low = mid_ref[base].astype(F32)
    high = mid_ref[base + 16].astype(F32)
    cols = cols_ref[...].astype(F32)
    return jnp.concatenate([cols * low, cols * high], axis=1)


def project(ref, t, gain, weights):
    rows = pl.ds(t * 256, 256)
    normed, rstd = norm(ref[rows, :].astype(F32), -1)
    both = nn((normed * gain).astype(BF), weights)
    return rows, normed, rstd, sigmoid(both[:, :128]), both[:, 128:]


class Fill:
    def __init__(self):
        self.todo = []

    def __call__(self, count=1):
        for work in self.todo[:count]:
            work()
        self.todo = self.todo[count:]


class Place:
    def __init__(self):
        row, col = lax.axis_index("row"), lax.axis_index("col")
        self.row, self.col = row, col
        self.x, self.yh = row // 2, lax.rem(row, 2)
        self.yl, self.z = col // 16, lax.rem(col // 2, 8)
        self.e = lax.rem(col, 2)

    def at(self, x=None, y=None, z=None, e=None):
        here = self.yh * 2 + self.yl
        y = here if y is None else lax.rem(here + y + 4, 4)
        x = self.x if x is None else lax.rem(self.x + x + 4, 4)
        z = self.z if z is None else lax.rem(self.z + z + 8, 8)
        e = self.e if e is None else 1 - self.e
        return (x * 2 + y // 2, lax.rem(y, 2) * 16 + z * 2 + e)

    def mate(self):
        return (self.row, (1 - self.yl) * 16 + self.z * 2 + self.e)

    def slot(self, same_y, dz):
        z = lax.rem(self.z + dz + 8, 8)
        yl = self.yl if same_y else 1 - self.yl
        return lax.rem(z, 2), yl * 4 + z // 2

    def across(self, same_y, dx):
        x = lax.rem(self.x + dx + 4, 4)
        yh = self.yh if same_y else 1 - self.yh
        return x * 2 + yh


def greet(place):
    barrier = pltpu.get_barrier_semaphore()
    partners = [
        place.at(e=1), place.at(z=1), place.at(z=-1), place.at(x=1), place.at(x=-1),
        place.at(y=1), place.at(y=-1),
    ]
    for partner in partners:
        pl.semaphore_signal(barrier, inc=1, device_id=partner, device_id_type=MESH)
    return lambda: pl.semaphore_wait(barrier, len(partners))


class Wire:
    def __init__(self, send, recv):
        self.send, self.recv = send, recv
        self.number, self.open = {}, []

    def copy(self, name, src, dst, to):
        index = self.number.setdefault(name, len(self.number))
        return pltpu.make_async_remote_copy(
            src_ref=src, dst_ref=dst, send_sem=self.send.at[index],
            recv_sem=self.recv.at[index], device_id=to, device_id_type=MESH,
        )

    def start(self, name, src, dst, to):
        made = self.copy(name, src, dst, to)
        made.start()
        self.open.append(made)

    def arrived(self, name, dst, to):
        self.copy(name, dst, dst, to).wait_recv()

    def finish(self):
        for made in self.open:
            made.wait_send()


PARTS = {"O0": (0, 32), "O1": (32, 32), "Y0": (0, 24), "Y1": (24, 24)}
LATE = (48, 16)


def gather_kernel(
    left_ref, right_ref, rows_ref, cols_ref, mid_ref, gain_ref, lg, lpw, rg, rpw,
    lp, rp, flat, turned_left, wide, right_bf, given, own, relay, send, recv, local,
):
    me = Place()
    wire = Wire(send, recv)
    met = greet(me)
    core, up, down, mate = me.at(e=1), me.at(z=1), me.at(z=-1), me.mate()
    east, west, north, south = me.at(x=1), me.at(x=-1), me.at(y=1), me.at(y=-1)
    low, high = pl.ds(0, 64), pl.ds(64, 64)
    base = me.e * 64
    gain = gain_ref[...]

    def channels(start, count):
        return pl.ds(pl.multiple_of(base + start, 8), count)

    def piece(same_y, dz, part=(0, 64)):
        kh, slot = me.slot(same_y, dz)
        return lp.at[kh, slot, channels(*part)]

    left_w = jnp.concatenate([lg[...], lpw[...]], axis=1)
    for t in range(4):
        rows, _, _, gate, value = project(left_ref, t, gain, left_w)
        flat[rows, :] = gate * value

    @pl.loop(0, 8, unroll=4)
    def _(k):
        part = flat[pl.ds(k, 128, stride=8), :].T
        turned_left[pl.ds(k, 128, stride=8), :] = part * left_mask(mid_ref, rows_ref, k)

    met()
    there = pl.ds(pl.multiple_of((1 - me.e) * 512, 512), 512)
    wire.start("core", turned_left.at[there], given, core)
    wire.arrived("core", given, core)

    @pl.loop(0, 8, unroll=2)
    def _(t):
        rows = pl.ds(pl.multiple_of(me.e * 512 + t * 64, 64), 64)
        ours = turned_left[rows, :].reshape(8, 8, 128)
        theirs = given[pl.ds(pl.multiple_of(t * 64, 64), 64), :].reshape(8, 8, 128)
        first = jnp.where(me.e == 0, ours, theirs)
        second = jnp.where(me.e == 0, theirs, ours)
        both = jnp.concatenate([first, second], axis=1)
        own[pl.ds(pl.multiple_of(t * 8, 8), 8)] = both.astype(BF)

    def from_own(name, part, to):
        wire.start(name, own.at[pl.ds(*part)], piece(True, 0, part), to)

    MATE = (("m0", (0, 24)), ("m1", (24, 24)), ("m2", LATE))
    for name in ("O0", "O1"):
        from_own("z+" + name + "1", PARTS[name], up)
        from_own("z-" + name + "1", PARTS[name], down)
        if name == "O0":
            for tag, part in MATE:
                from_own(tag, part, mate)
    keep_left = pltpu.make_async_copy(own, piece(True, 0), local.at[1])
    keep_left.start()
    from_own("cO0", (0, 64), core)

    right_w = jnp.concatenate([rg[...], rpw[...]], axis=1)

    def right_rows(t):
        rows, _, _, gate, value = project(right_ref, t, gain, right_w)
        flat[rows, :] = gate * value

    def right_turn():
        @pl.loop(0, 16, unroll=4)
        def _(k):
            first = flat[pl.ds(k, 64, stride=32), :]
            second = flat[pl.ds(k + 16, 64, stride=32), :]
            part = jnp.concatenate([first, second], axis=0).T
            wide[pl.ds(k, 128, stride=16), :] = part * right_mask(mid_ref, cols_ref, k)

        @pl.loop(0, 16, unroll=4)
        def _(t):
            rows = pl.ds(pl.multiple_of(t * 128, 128), 128)
            part = wide[rows, :].reshape(8, 16, 128).astype(BF)
            right_bf[pl.ds(pl.multiple_of(t * 8, 8), 8)] = part

    def share(name, same_y, dz):
        wire.start("c" + name, piece(same_y, dz), piece(same_y, dz), core)

    def mate_part(index):
        tag, part = MATE[index]
        wire.arrived(tag, piece(False, 0, part), mate)
        if index < 2:
            name = "Y" + str(index)
            ref = piece(False, 0, part)
            wire.start("z+" + name + "1", ref, ref, up)
            wire.start("z-" + name + "1", ref, ref, down)
        else:
            share("Y0", False, 0)

    def left_step(name, d):
        same = name[0] == "O"
        part = PARTS[name]
        for sign, dz, to, last in (("z+", -d, up, "0"), ("z-", d, down, "1")):
            if d == 4 and name[1] != last:
                continue
            ref = piece(same, dz, part)
            wire.arrived(sign + name + str(d), ref, to)
            if d < 3 or (d == 3 and name[1] == last):
                wire.start(sign + name + str(d + 1), ref, ref, to)
        if name == "O1":
            for dz in (-d, d)[d // 4:]:
                ref = piece(True, dz, LATE)
                wire.start("y" + str(dz), ref, ref, mate)
                share("O" + str(dz), True, dz)

    def late(d):
        for dz in (-d, d)[d // 4:]:
            wire.arrived("y" + str(dz), piece(False, dz, LATE), mate)
            share("Y" + str(dz), False, dz)

    def right_send(src, tag):
        to = rp.at[me.across(tag == "", 0)]
        for name, part, way in (
            ("x+a", low, east), ("x-b", high, west), ("x+b", high, east), ("x-a", low, west),
        ):
            wire.start(name + tag + "1", src.at[part], to.at[part], way)

    def right_step(tag):
        behind, ahead = rp.at[me.across(tag == "", -1)], rp.at[me.across(tag == "", 1)]
        wire.arrived("x+a" + tag + "1", behind.at[low], east)
        wire.start("x+a" + tag + "2", behind.at[low], behind.at[low], east)
        wire.arrived("x-b" + tag + "1", ahead.at[high], west)
        wire.start("x-b" + tag + "2", ahead.at[high], ahead.at[high], west)

    def right_rest(tag):
        behind, ahead = rp.at[me.across(tag == "", -1)], rp.at[me.across(tag == "", 1)]
        far = rp.at[me.across(tag == "", 2)]
        wire.arrived("x+b" + tag + "1", behind.at[high], east)
        wire.arrived("x-a" + tag + "1", ahead.at[low], west)
        wire.arrived("x+a" + tag + "2", far.at[low], east)
        wire.arrived("x-b" + tag + "2", far.at[high], west)

    for t in range(3):
        right_rows(t)
    mate_part(0)
    left_step("O0", 1)
    mate_part(1)
    for t in range(3, 6):
        right_rows(t)
    left_step("O1", 1)
    mate_part(2)
    for t in range(6, 8):
        right_rows(t)
    right_turn()
    keep_right = pltpu.make_async_copy(right_bf, rp.at[me.row], local.at[0])
    right_send(right_bf, "")
    wire.start("ya", right_bf.at[low], relay.at[0], north)
    wire.start("yb", right_bf.at[high], relay.at[1], south)
    keep_right.start()
    left_step("Y0", 1)
    left_step("O0", 2)
    left_step("Y1", 1)
    left_step("O1", 2)
    late(1)
    left_step("Y0", 2)
    above, below = lax.rem(me.yh * 2 + me.yl + 3, 4), lax.rem(me.yh * 2 + me.yl + 1, 4)
    wire.arrived("ya", relay.at[0], north)
    wire.start("ya2", relay.at[0], rp.at[me.x * 2 + above // 2, low], north)
    wire.arrived("yb", relay.at[1], south)
    wire.start("yb2", relay.at[1], rp.at[me.x * 2 + below // 2, high], south)
    left_step("Y1", 2)
    right_step("")
    left_step("O0", 3)
    left_step("O1", 3)
    late(2)
    pair = rp.at[me.across(False, 0)]
    wire.arrived("ya2", pair.at[low], north)
    wire.arrived("yb2", pair.at[high], south)
    right_send(pair, "p")
    left_step("Y0", 3)
    left_step("Y1", 3)
    left_step("O0", 4)
    left_step("O1", 4)
    late(3)
    right_step("p")
    right_rest("")
    left_step("Y0", 4)
    left_step("Y1", 4)
    late(4)
    right_rest("p")
    base = (1 - me.e) * 64
    for src in ("O", "Y"):
        for dz in (0, -1, 1, -2, 2, -3, 3, 4):
            wire.arrived("c" + src + str(dz), piece(src == "O", dz), core)
    keep_right.wait()
    keep_left.wait()
    wire.finish()


def gather(*operands):
    return pl.pallas_call(
        gather_kernel,
        out_shape=(
            jax.ShapeDtypeStruct((2, 8, 128, 16, 128), BF),
            jax.ShapeDtypeStruct((8, 128, 16, 128), BF),
        ),
        in_specs=[VMEM] * 4 + [SMEM] + [VMEM] * 5,
        out_specs=(ANY, ANY),
        scratch_shapes=[
            pltpu.VMEM((2048, 128), F32),
            pltpu.VMEM((1024, 128), F32),
            pltpu.VMEM((2048, 128), F32),
            pltpu.VMEM((128, 16, 128), BF),
            pltpu.VMEM((512, 128), F32),
            pltpu.VMEM((64, 16, 128), BF),
            pltpu.VMEM((2, 64, 16, 128), BF),
            pltpu.SemaphoreType.DMA((80,)),
            pltpu.SemaphoreType.DMA((80,)),
            pltpu.SemaphoreType.DMA((2,)),
        ],
        compiler_params=pltpu.CompilerParams(
            collective_id=0, has_side_effects=True, vmem_limit_bytes=LIMIT
        ),
        name="gather_panels",
    )(*operands)


def scatter_kernel(
    dl, dr, left_ref, right_ref, rows_ref, cols_ref, mid_ref, gain_ref, lg, lpw, rg, rpw,
    left_out, right_out,
    ls, core_in, z_in, late_in, mate_in, give, got, rs, x_in, relay, pair_in,
    flat_left, flat_right, back, norms, rstds, gates, values,
    send, recv, local,
):
    me = Place()
    wire = Wire(send, recv)
    met = greet(me)
    core, up, down, mate = me.at(e=1), me.at(z=1), me.at(z=-1), me.mate()
    east, west, north, south = me.at(x=1), me.at(x=-1), me.at(y=1), me.at(y=-1)
    low, high = pl.ds(0, 64), pl.ds(64, 64)
    half = pl.ds(pl.multiple_of(me.e * 64, 64), 64)
    other = pl.ds(pl.multiple_of((1 - me.e) * 64, 64), 64)
    gain = gain_ref[...]

    loads = {}

    def load(key, src, dst):
        made = pltpu.make_async_copy(src, dst, local.at[len(loads)])
        made.start()
        loads[key] = made

    for which in (0, 1):
        load(("r", which, 2), dr.at[me.across(which == 1, 2)], rs.at[which, 2])
    for dz in (4, 3, 5, 2, 6, 1, 7, 0):
        for which in (0, 1):
            kh, slot = me.slot(which == 1, dz)
            load((which, dz), dl.at[kh, slot, half], ls.at[which, dz])
    met()
    for count, dz in enumerate((4, 3, 5, 2, 6, 1, 7, 0)):
        for which in (0, 1):
            kh, slot = me.slot(which == 1, dz)
            wire.start(f"c{which}{dz}", dl.at[kh, slot, other], core_in.at[which, dz], core)
        if count < 3:
            dx = (1, 3, 0)[count]
            for which in (0, 1):
                load(("r", which, dx), dr.at[me.across(which == 1, dx)], rs.at[which, dx])

    fill = Fill()
    left_w = jnp.concatenate([lg[...], lpw[...]], axis=1)
    right_w = jnp.concatenate([rg[...], rpw[...]], axis=1)

    def ahead(ref, t, weights, shift):
        def work():
            _, normed, rstd, gate, value = project(ref, t, gain, weights)
            rows = pl.ds(shift + t * 256, 256)
            norms[rows, :] = normed
            rstds[rows, :] = jnp.broadcast_to(rstd, (256, 128))
            gates[rows, :] = gate
            values[rows, :] = value * gate * (1.0 - gate)

        return work

    for t in range(8):
        fill.todo.append(ahead(right_ref, t, right_w, 1024))
    for t in range(4):
        fill.todo.append(ahead(left_ref, t, left_w, 0))

    def side_back(count, weights, shift, out):
        for t in range(count):
            here, rows = pl.ds(t * 256, 256), pl.ds(shift + t * 256, 256)
            masked = back[here, :]
            d_value = (masked * gates[rows, :]).astype(BF)
            d_gate = (masked * values[rows, :]).astype(BF)
            d_norm = nt(jnp.concatenate([d_gate, d_value], axis=1), weights)
            result = norm_back(norms[rows, :], rstds[rows, :], gain, d_norm, -1)
            out[here, :] = result.astype(BF)

    def add(target, start, count, terms, out=None):
        @pl.loop(0, count // 8, unroll=2)
        def _(t):
            part = pl.ds(pl.multiple_of(start + t * 8, 8), 8)
            total = target[part].astype(F32)
            for term, shift in terms:
                place = pl.ds(pl.multiple_of(start - shift + t * 8, 8), 8)
                total = total + term[place].astype(F32)
            if out is None:
                target[part] = total.astype(BF)
            else:
                out(start // 8 + t, total)

    def ready(which, dz):
        loads[which, dz].wait()
        wire.arrived(f"c{which}{dz}", core_in.at[which, dz], core)
        if which == 0:
            start, count = LATE
            add(ls.at[0, dz], start, count, [(core_in.at[0, dz], 0)])
            wire.start(f"l{dz}", ls.at[0, dz, pl.ds(*LATE)], late_in.at[dz], mate)
        else:
            wire.arrived(f"l{dz}", late_in.at[dz], mate)

    def send_part(name, way, dz, d, more):
        which = 1 if name[0] == "O" else 0
        start, count = PARTS[name]
        block = ls.at[which, dz]
        terms = [(core_in.at[which, dz], 0)] + more
        if name == "O1":
            add(block, start, 16, terms)
            add(block, LATE[0], LATE[1], terms + [(late_in.at[dz], LATE[0])])
        else:
            add(block, start, count, terms)
        part = pl.ds(start, count)
        sign, to = (("+", up), ("-", down))[way]
        wire.start(f"z{sign}{name}{d}", block.at[part], z_in.at[way, which, d, part], to)

    def came(name, way, d):
        which = 1 if name[0] == "O" else 0
        sign, to = (("+", up), ("-", down))[way]
        ref = z_in.at[way, which, d]
        wire.arrived(f"z{sign}{name}{d}", ref.at[pl.ds(*PARTS[name])], to)
        return [(ref, 0)]

    def left_step(which, d):
        names = ("O0", "O1") if which else ("Y0", "Y1")
        if d == 0:
            ready(which, 4)
            for way in (0, 1):
                send_part(names[way], way, 4, 0, [])
            return
        ready(which, 4 - d)
        ready(which, 4 + d)
        for name in names:
            for way in (0, 1):
                dz = 4 + d if way else 4 - d
                more = came(name, way, d - 1) if d > 1 or name[1] == str(way) else []
                send_part(name, way, dz, d, more)

    def right_first(which):
        loads["r", which, 2].wait()
        block = rs.at[which, 2]
        wire.start(f"x+{which}0", block.at[low], x_in.at[0, which, 0, low], east)
        wire.start(f"x-{which}0", block.at[high], x_in.at[1, which, 0, high], west)

    def right_step(which):
        for way, sign, to, dx, part in (
            (0, "+", east, 1, low), (1, "-", west, 3, high),
        ):
            loads["r", which, dx].wait()
            ref, block = x_in.at[way, which, 0], rs.at[which, dx]
            wire.arrived(f"x{sign}{which}0", ref.at[part], to)
            add(block, way * 64, 64, [(ref, 0)])
            wire.start(f"x{sign}{which}1", block, x_in.at[way, which, 1], to)

    def right_last(which):
        loads["r", which, 0].wait()
        wire.arrived(f"x+{which}1", x_in.at[0, which, 1], east)
        wire.arrived(f"x-{which}1", x_in.at[1, which, 1], west)
        return [(x_in.at[0, which, 1], 0), (x_in.at[1, which, 1], 0)]

    right_first(0)
    right_first(1)
    left_step(0, 0)
    left_step(1, 0)
    right_step(0)
    fill(1)
    left_step(0, 1)
    left_step(1, 1)
    fill(2)
    right_step(1)
    fill(2)
    left_step(0, 2)
    fill(2)
    left_step(1, 2)
    fill(2)
    add(rs.at[0, 0], 0, 128, right_last(0))
    wire.start("ya", rs.at[0, 0, low], relay.at[0], north)
    wire.start("yb", rs.at[0, 0, high], relay.at[1], south)
    left_step(0, 3)
    fill(2)
    left_step(1, 3)
    wire.arrived("ya", relay.at[0], north)
    wire.start("ya2", relay.at[0], pair_in.at[low], north)
    wire.arrived("yb", relay.at[1], south)
    wire.start("yb2", relay.at[1], pair_in.at[high], south)
    fill(4)
    ready(0, 0)
    ready(1, 0)
    terms = [(core_in.at[0, 0], 0)]
    for name in ("Y0", "Y1"):
        start, count = PARTS[name]
        more = came(name, 0, 3) + came(name, 1, 3)
        add(ls.at[0, 0], start, count, terms + more)
    wire.start("mate", ls.at[0, 0, pl.ds(0, 48)], mate_in, mate)

    def put_left(t, total):
        first, second = total[:, :8].reshape(64, 128), total[:, 8:].reshape(64, 128)
        rows = pl.ds(pl.multiple_of(me.e * 512 + t * 64, 64), 64)
        flat_left[rows, :] = jnp.where(me.e == 0, first, second)
        give[pl.ds(pl.multiple_of(t * 64, 64), 64), :] = jnp.where(me.e == 0, second, first)

    terms = [(core_in.at[1, 0], 0), (mate_in, 0)]
    wire_terms = came("O0", 0, 3) + came("O0", 1, 3)
    came("O1", 0, 3)
    came("O1", 1, 3)
    wire.arrived("mate", mate_in, mate)
    add(ls.at[1, 0], 0, 48, terms + wire_terms, put_left)
    terms = [(core_in.at[1, 0], 0), (late_in.at[0], LATE[0])]
    add(ls.at[1, 0], LATE[0], LATE[1], terms + wire_terms, put_left)
    wire.start("last", give, got, core)

    terms = right_last(1)
    wire.arrived("ya2", pair_in.at[low], north)
    wire.arrived("yb2", pair_in.at[high], south)

    def put_right(t, total):
        rows = pl.ds(pl.multiple_of(t * 128, 128), 128)
        flat_right[rows, :] = total.reshape(128, 128)

    add(rs.at[1, 0], 0, 128, terms + [(pair_in, 0)], put_right)

    @pl.loop(0, 16, unroll=4)
    def _(k):
        rows = flat_right[pl.ds(k, 128, stride=16), :] * right_mask(mid_ref, cols_ref, k)
        turned = rows.T
        back[pl.ds(k, 64, stride=32), :] = turned[:64, :]
        back[pl.ds(k + 16, 64, stride=32), :] = turned[64:, :]

    side_back(8, right_w, 1024, right_out)

    wire.arrived("last", got, core)
    flat_left[pl.ds(pl.multiple_of((1 - me.e) * 512, 512), 512), :] = got[...]

    @pl.loop(0, 8, unroll=4)
    def _(k):
        rows = flat_left[pl.ds(k, 128, stride=8), :] * left_mask(mid_ref, rows_ref, k)
        back[pl.ds(k, 128, stride=8), :] = rows.T

    side_back(4, left_w, 0, left_out)
    wire.finish()


def scatter(*operands):
    return pl.pallas_call(
        scatter_kernel,
        out_shape=(
            jax.ShapeDtypeStruct((1024, 128), BF),
            jax.ShapeDtypeStruct((2048, 128), BF),
        ),
        in_specs=[ANY, ANY] + [VMEM] * 4 + [SMEM] + [VMEM] * 5,
        out_specs=(VMEM, VMEM),
        scratch_shapes=[
            pltpu.VMEM((2, 8, 64, 16, 128), BF),
            pltpu.VMEM((2, 8, 64, 16, 128), BF),
            pltpu.VMEM((2, 2, 4, 64, 16, 128), BF),
            pltpu.VMEM((8, 16, 16, 128), BF),
            pltpu.VMEM((48, 16, 128), BF),
            pltpu.VMEM((512, 128), F32),
            pltpu.VMEM((512, 128), F32),
            pltpu.VMEM((2, 4, 128, 16, 128), BF),
            pltpu.VMEM((2, 2, 2, 128, 16, 128), BF),
            pltpu.VMEM((2, 64, 16, 128), BF),
            pltpu.VMEM((128, 16, 128), BF),
            pltpu.VMEM((1024, 128), F32),
            pltpu.VMEM((2048, 128), F32),
            pltpu.VMEM((2048, 128), F32),
            pltpu.VMEM((3072, 128), F32),
            pltpu.VMEM((3072, 128), F32),
            pltpu.VMEM((3072, 128), F32),
            pltpu.VMEM((3072, 128), F32),
            pltpu.SemaphoreType.DMA((80,)),
            pltpu.SemaphoreType.DMA((80,)),
            pltpu.SemaphoreType.DMA((24,)),
        ],
        compiler_params=pltpu.CompilerParams(
            collective_id=1, has_side_effects=True, vmem_limit_bytes=LIMIT
        ),
        name="scatter_sums",
    )(*operands)


CS = 16
NC = 128 // CS
JS = 8
NJ = 64 // JS


def middle_kernel(
    lp, rp, tile_ref, up_ref, in_gain_ref, gate_w_ref, mid_gain_ref, proj_w_ref,
    update_ref, d_tile_ref, dl_ref, dr_ref, tri, flat,
):
    step = pl.program_id(0)

    @pl.when(step < NC)
    def _():
        for c in range(CS):
            right = rp[:, c].reshape(128, 128)
            turned = right.T
            sides = jnp.concatenate([turned[:64], turned[64:]], axis=1)
            left = jnp.concatenate(
                [lp[0, :, c].reshape(128, 128), lp[1, :, c].reshape(128, 128)], axis=0
            )
            result = nn(sides, left)
            rows = pl.ds(pl.multiple_of((step * CS + c) * 8, 8), 8)
            for block in range(NJ):
                tri[block, rows, :] = result[block * 8:(block + 1) * 8]

    @pl.when((step >= NC) & (step < NC + NJ))
    def _():
        block = tri.at[step - NC]
        mid_gain = jnp.broadcast_to(mid_gain_ref[...], (128, 128)).T
        in_gain = in_gain_ref[...]
        proj_w = proj_w_ref[...]
        gate_w = gate_w_ref[...]

        for j in range(JS):
            normed, _ = norm(block[pl.ds(j, 128, stride=8), :], 0)
            value = tn((normed * mid_gain).astype(BF), proj_w)
            flat[pl.ds(j, 128, stride=8), :] = value

        for t in range(8):
            rows = pl.ds(t * 128, 128)
            items = pl.ds(t * 16, 16)
            tile = tile_ref[items].astype(F32).reshape(128, 128)
            upstream = up_ref[items].astype(F32).reshape(128, 128)
            normed, rstd = norm(tile, -1)
            gate = sigmoid(nn((normed * in_gain).astype(BF), gate_w))
            value = flat[rows, :]
            update_ref[items] = (gate * value).reshape(16, 8, 128).astype(BF)
            gated = upstream * gate
            flat[rows, :] = gated
            d_gate = (gated * value * (1.0 - gate)).astype(BF)
            d_norm = nt(d_gate, gate_w)
            d_tile = norm_back(normed, rstd, in_gain, d_norm, -1)
            d_tile_ref[items] = d_tile.reshape(16, 8, 128).astype(BF)

        for j in range(JS):
            here = pl.ds(j, 128, stride=8)
            normed, rstd = norm(block[here, :], 0)
            d_norm = nt(proj_w, flat[here, :].astype(BF))
            block[here, :] = norm_back(normed, rstd, mid_gain, d_norm, 0)

    @pl.when(step >= NC + NJ)
    def _():
        for c in range(CS):
            rows = pl.ds(pl.multiple_of(((step - NC - NJ) * CS + c) * 8, 8), 8)
            grad = jnp.concatenate(
                [tri[block, rows, :] for block in range(NJ)], axis=0
            ).astype(BF)
            none = jnp.zeros((64, 128), BF)
            grad = jnp.concatenate(
                [
                    jnp.concatenate([grad, none], axis=1),
                    jnp.concatenate([none, grad], axis=1),
                ],
                axis=0,
            )
            right = rp[:, c].reshape(128, 128)
            left = jnp.concatenate(
                [lp[0, :, c].reshape(128, 128), lp[1, :, c].reshape(128, 128)], axis=1
            )
            d_left = nn(right, grad).astype(BF)
            dl_ref[0, :, c] = d_left[:, :128].reshape(8, 16, 128)
            dl_ref[1, :, c] = d_left[:, 128:].reshape(8, 16, 128)
            dr_ref[:, c] = nt(left, grad).astype(BF).reshape(8, 16, 128)


def middle(lp, rp, tile, upstream, in_gain, gate_w, mid_gain, proj_w):
    def channel(s):
        return jnp.where(s < NC + NJ, jnp.minimum(s, NC - 1), s - NC - NJ)

    def column(s):
        return jnp.clip(s - NC, 0, NJ - 1)

    def later(s):
        return jnp.maximum(s - NC - NJ, 0)

    left = lambda at: pl.BlockSpec((2, 8, CS, 16, 128), lambda s: (0, 0, at(s), 0, 0))
    right = lambda at: pl.BlockSpec((8, CS, 16, 128), lambda s: (0, at(s), 0, 0))
    cell = pl.BlockSpec((128, JS, 128), lambda s: (0, column(s), 0))
    whole = pl.BlockSpec((128, 128), lambda s: (0, 0))
    line = pl.BlockSpec((1, 128), lambda s: (0, 0))
    return pl.pallas_call(
        middle_kernel,
        grid=(NC + NJ + NC,),
        out_shape=(
            jax.ShapeDtypeStruct((128, 64, 128), BF),
            jax.ShapeDtypeStruct((128, 64, 128), BF),
            jax.ShapeDtypeStruct((2, 8, 128, 16, 128), BF),
            jax.ShapeDtypeStruct((8, 128, 16, 128), BF),
        ),
        in_specs=[left(channel), right(channel), cell, cell, line, whole, line, whole],
        out_specs=(cell, cell, left(later), right(later)),
        scratch_shapes=[
            pltpu.VMEM((NJ, 1024, 128), F32),
            pltpu.VMEM((1024, 128), F32),
        ],
        compiler_params=pltpu.CompilerParams(
            vmem_limit_bytes=LIMIT, dimension_semantics=("arbitrary",)
        ),
        name="middle",
    )(lp, rp, tile, upstream, in_gain, gate_w, mid_gain, proj_w)


def body(
    pair_left,
    pair_right,
    pair_tile,
    d_update,
    mask_rows,
    mask_cols,
    mask_mid,
    ln_in_gain,
    left_gate_w,
    left_proj_w,
    right_gate_w,
    right_proj_w,
    out_gate_w,
    ln_mid_gain,
    out_proj_w,
):
    flat_left = pair_left.reshape(1024, 128)
    flat_right = pair_right.reshape(2048, 128)
    gain = ln_in_gain.reshape(1, 128)
    sides = (
        flat_left, flat_right, mask_rows.reshape(1, 128), mask_cols.reshape(1, 64),
        mask_mid, gain, left_gate_w, left_proj_w, right_gate_w, right_proj_w,
    )
    lp, rp = gather(*sides)
    update, d_tile, dl, dr = middle(
        lp, rp, pair_tile, d_update, gain, out_gate_w, ln_mid_gain.reshape(1, 128),
        out_proj_w,
    )
    d_left, d_right = scatter(dl, dr, *sides)
    return (
        update,
        d_left.reshape(128, 8, 128),
        d_right.reshape(64, 32, 128),
        d_tile,
    )


def solution(mesh):
    in_specs = (
        P("row", "col", None),
        P("col", "row", None),
        P("row", "col", None),
        P("row", "col", None),
        P("row"),
        P("col"),
        P(),
        P(),
        P(),
        P(),
        P(),
        P(),
        P(),
        P(),
        P(),
    )
    out_specs = (
        P("row", "col", None),
        P("row", "col", None),
        P("col", "row", None),
        P("row", "col", None),
    )
    return jax.shard_map(body, mesh=mesh, in_specs=in_specs, out_specs=out_specs, check_vma=False)
```

time: 176 us -> 160 us (0.909)
  Pallas kernels: 172 us -> 156 us
  local copies, waits for them, and re-layouts: 1.37 us -> 3.54 us
    pallas_call x3 -> x1, Pallas kernels: 75.7 us -> 55.9 us  [scatter(): pl.pallas_call(scatter_kernel, out_shape=(jax.ShapeDtypeStruct((1024, 128...]
    unnamed x0 -> x2, local copies, waits for them, and re-layouts: none -> 3.54 us
    pallas_call x1, Pallas kernels: 61.4 us -> 64.5 us  [gather(): pl.pallas_call(gather_kernel, out_shape=(jax.ShapeDtypeStruct((2, 8, 128,...]
where the time goes in v2:
time: 160 us
  Pallas kernels  156 us (98%)
  local copies, waits for them, and re-layouts  3.54 us (2%)
    pallas_call x1, Pallas kernels, gather(): pl.pallas_call(gather_kernel, out_shape=(jax.ShapeDtypeStruct((2, 8, 128,...  64.5 us
    pallas_call x1, Pallas kernels, scatter(): pl.pallas_call(scatter_kernel, out_shape=(jax.ShapeDtypeStruct((1024, 128...  55.9 us
    pallas_call x1, Pallas kernels, middle(): pl.pallas_call(middle_kernel, grid=(NC + NJ + NC,), out_shape=(jax.ShapeD...  35.4 us
    unnamed x2, local copies, waits for them, and re-layouts  3.54 us

profile of v2, /device:TPU:1, one launch (start us, length us, event | category | flops | bytes accessed | tf_op | source)
XLA Modules:
  0.0 160.0 jit_solution(4006371164490513265)
XLA Ops:
  0.6 64.5 %gather_panels.1 = (bf16[2,8,128,16,128]{4,3,2,1,0:T(8,128)(2,1)}, bf16[8,128,16,128]{3,2,1,0:T(8,128)(2,1)}) custom-call(bf16[1024,128]{1,0:T(8,128)(2,1)} %bitcast.10, bf16[2048,128]{1,0:T(8,128)(2,1)} %bitcast.8, s32[1,128]{1,0:T(1,128)} %bitcast.17, s32[1,64]{1,0:T(1,128)} %bitcast.19, s32[256]{0:T(256)} %mid_ref.3, f32[1,128]{1,0:T(1,128)} %bitcast.14, ...), custom_call_target="tpu_custom_call" | custom-call | tf_op jit(solution)/shard_map/gather_panels/pallas_call | solution.py:341
  65.1 35.4 %middle.1 = (bf16[128,64,128]{2,1,0:T(8,128)(2,1)}, bf16[128,64,128]{2,1,0:T(8,128)(2,1)}, bf16[2,8,128,16,128]{4,3,2,1,0:T(8,128)(2,1)}, bf16[8,128,16,128]{3,2,1,0:T(8,128)(2,1)}) custom-call(bf16[2,8,128,16,128]{4,3,2,1,0:T(8,128)(2,1)} %get-tuple-element.12.lp, bf16[8,128,16,128]{3,2,1,0:T(8,128)(2,1)} %get-tuple-element.13.rp, ...), custom_call_target="tpu_custom_call" | custom-call | tf_op jit(solution)/shard_map/middle/pallas_call | solution.py:741
  100.5 55.9 %scatter_sums.1 = (bf16[1024,128]{1,0:T(8,128)(2,1)}, bf16[2048,128]{1,0:T(8,128)(2,1)}) custom-call(bf16[2,8,128,16,128]{4,3,2,1,0:T(8,128)(2,1)} %get-tuple-element.15.dl, bf16[8,128,16,128]{3,2,1,0:T(8,128)(2,1)} %get-tuple-element.16.dr, bf16[1024,128]{1,0:T(8,128)(2,1)} %bitcast.11, bf16[2048,128]{1,0:T(8,128)(2,1)} %bitcast.9, s32[1,128]{1,0:T(1,128)} %bitcast.18, ...), custom_call_target="tpu_custom_call" | custom-call | tf_op jit(solution)/shard_map/scatter_sums/pallas_call | solution.py:602
  156.4 1.7 %copy.21 = bf16[128,8,128]{2,1,0:T(8,128)(2,1)} copy(bf16[128,8,128]{2,1,0:T(8,128)(2,1)} %bitcast.13) | data formatting | bytes 524288
  158.1 1.9 %copy.22 = bf16[64,32,128]{2,1,0:T(8,128)(2,1)} copy(bf16[64,32,128]{2,1,0:T(8,128)(2,1)} %bitcast.12) | data formatting | bytes 1048576

commit v3 on v0

v3 whole, which is shorter than its diff:
```python
import functools

import jax
import jax.numpy as jnp
from jax import lax
from jax.experimental import pallas as pl
from jax.experimental.pallas import tpu as pltpu
from jax.sharding import PartitionSpec as P

MESH = pl.DeviceIdType.MESH
BF = jnp.bfloat16
F32 = jnp.float32
VMEM = pl.BlockSpec(memory_space=pltpu.VMEM)
SMEM = pl.BlockSpec(memory_space=pltpu.SMEM)
ANY = pl.BlockSpec(memory_space=pl.ANY)
LIMIT = 60 * 1024 * 1024


def nn(a, b):
    return lax.dot_general(a, b, (((1,), (0,)), ((), ())), preferred_element_type=F32)


def nt(a, b):
    return lax.dot_general(a, b, (((1,), (1,)), ((), ())), preferred_element_type=F32)


def tn(a, b):
    return lax.dot_general(a, b, (((0,), (0,)), ((), ())), preferred_element_type=F32)


def sigmoid(v):
    return 0.5 * jnp.tanh(0.5 * v) + 0.5


def norm(values, axis):
    centred = values - jnp.mean(values, axis=axis, keepdims=True)
    rstd = lax.rsqrt(jnp.mean(centred * centred, axis=axis, keepdims=True) + 1e-05)
    return centred * rstd, rstd


def norm_back(normed, rstd, gain, upstream, axis):
    scaled = upstream * gain
    inner = jnp.mean(scaled * normed, axis=axis, keepdims=True)
    return (scaled - jnp.mean(scaled, axis=axis, keepdims=True) - normed * inner) * rstd


def left_mask(mid_ref, rows_ref, k):
    keep = mid_ref[lax.axis_index("col") * 8 + k].astype(F32)
    return rows_ref[...].astype(F32) * keep


def right_mask(mid_ref, cols_ref, k):
    base = lax.axis_index("row") * 32 + k
    low = mid_ref[base].astype(F32)
    high = mid_ref[base + 16].astype(F32)
    cols = cols_ref[...].astype(F32)
    return jnp.concatenate([cols * low, cols * high], axis=1)


def project(ref, t, gain, weights):
    rows = pl.ds(t * 256, 256)
    normed, rstd = norm(ref[rows, :].astype(F32), -1)
    both = nn((normed * gain).astype(BF), weights)
    return rows, normed, rstd, sigmoid(both[:, :128]), both[:, 128:]


class Fill:
    def __init__(self):
        self.todo = []

    def __call__(self, count=1):
        for work in self.todo[:count]:
            work()
        self.todo = self.todo[count:]


class Place:
    def __init__(self):
        row, col = lax.axis_index("row"), lax.axis_index("col")
        self.row, self.col = row, col
        self.x, self.yh = row // 2, lax.rem(row, 2)
        self.yl, self.z = col // 16, lax.rem(col // 2, 8)
        self.e = lax.rem(col, 2)

    def at(self, x=None, y=None, z=None, e=None):
        here = self.yh * 2 + self.yl
        y = here if y is None else lax.rem(here + y + 4, 4)
        x = self.x if x is None else lax.rem(self.x + x + 4, 4)
        z = self.z if z is None else lax.rem(self.z + z + 8, 8)
        e = self.e if e is None else 1 - self.e
        return (x * 2 + y // 2, lax.rem(y, 2) * 16 + z * 2 + e)

    def mate(self):
        return (self.row, (1 - self.yl) * 16 + self.z * 2 + self.e)

    def slot(self, same_y, dz):
        z = lax.rem(self.z + dz + 8, 8)
        yl = self.yl if same_y else 1 - self.yl
        return lax.rem(z, 2), yl * 4 + z // 2

    def across(self, same_y, dx):
        x = lax.rem(self.x + dx + 4, 4)
        yh = self.yh if same_y else 1 - self.yh
        return x * 2 + yh


def greet(place):
    barrier = pltpu.get_barrier_semaphore()
    partners = [
        place.at(e=1), place.at(z=1), place.at(z=-1), place.at(x=1), place.at(x=-1),
        place.at(y=1), place.at(y=-1),
    ]
    for partner in partners:
        pl.semaphore_signal(barrier, inc=1, device_id=partner, device_id_type=MESH)
    return lambda: pl.semaphore_wait(barrier, len(partners))


class Wire:
    def __init__(self, send, recv):
        self.send, self.recv = send, recv
        self.number, self.open = {}, []

    def copy(self, name, src, dst, to):
        index = self.number.setdefault(name, len(self.number))
        return pltpu.make_async_remote_copy(
            src_ref=src, dst_ref=dst, send_sem=self.send.at[index],
            recv_sem=self.recv.at[index], device_id=to, device_id_type=MESH,
        )

    def start(self, name, src, dst, to):
        made = self.copy(name, src, dst, to)
        made.start()
        self.open.append(made)

    def arrived(self, name, dst, to):
        self.copy(name, dst, dst, to).wait_recv()

    def finish(self):
        for made in self.open:
            made.wait_send()


def part_of(name, group):
    return (32 * group, 32 if name == "O" else 24)


def late_of(group):
    return (32 * group + 24, 8)


def halves_of(name, group):
    start, count = part_of(name, group)
    return (start, 16), (start + 16, count - 16)


def group_rows(group):
    return pl.ds(32 * group, 32), pl.ds(64 + 32 * group, 32)


def gather_kernel(
    left_ref, right_ref, rows_ref, cols_ref, mid_ref, gain_ref, lg, lpw, rg, rpw,
    lp_out, rp_out, tri_out, lp, rp, tri, flat, turned, turned_left, given, relay, send, recv, local,
):
    me = Place()
    wire = Wire(send, recv)
    met = greet(me)
    core, up, down, mate = me.at(e=1), me.at(z=1), me.at(z=-1), me.mate()
    east, west, north, south = me.at(x=1), me.at(x=-1), me.at(y=1), me.at(y=-1)
    gain = gain_ref[...]
    outs = []

    def channels(start, count, half):
        return pl.ds(pl.multiple_of(half * 64 + start, 8), count)

    def piece(same_y, dz, part, half=None):
        kh, slot = me.slot(same_y, dz)
        return lp.at[kh, slot, channels(*part, me.e if half is None else half)]

    def normed_rows(ref, t):
        rows = pl.ds(t * 256, 256)
        normed, _ = norm(ref[rows, :].astype(F32), -1)
        flat[rows, :] = normed * gain

    def gated(weights, rows, mask):
        both = nt(weights, rows.astype(BF))
        return sigmoid(both[:128]) * both[128:] * mask

    left_w = jnp.concatenate([lg[...].T, lpw[...].T], axis=0)
    for t in range(4):
        normed_rows(left_ref, t)

    @pl.loop(0, 8, unroll=4)
    def _(k):
        rows = flat[pl.ds(k, 128, stride=8), :]
        turned_left[pl.ds(k, 128, stride=8), :] = gated(
            left_w, rows, left_mask(mid_ref, rows_ref, k)
        )

    met()
    there = pl.ds(pl.multiple_of((1 - me.e) * 512, 512), 512)
    wire.start("core", turned_left.at[there], given, core)
    wire.arrived("core", given, core)
    own_kh, own_slot = me.slot(True, 0)

    @pl.loop(0, 8, unroll=2)
    def _(t):
        rows = pl.ds(pl.multiple_of(me.e * 512 + t * 64, 64), 64)
        ours = turned_left[rows, :].reshape(8, 8, 128)
        theirs = given[pl.ds(pl.multiple_of(t * 64, 64), 64), :].reshape(8, 8, 128)
        first = jnp.where(me.e == 0, ours, theirs)
        second = jnp.where(me.e == 0, theirs, ours)
        both = jnp.concatenate([first, second], axis=1)
        lp[own_kh, own_slot, channels(t * 8, 8, me.e)] = both.astype(BF)

    def copy(name, ref, to):
        wire.start(name, ref, ref, to)

    def left_send(g):
        ref = piece(True, 0, part_of("O", g))
        copy(f"z+O{g}1", ref, up)
        copy(f"z-O{g}1", ref, down)
        copy(f"m{g}", ref, mate)
        copy(f"cO{g}0", ref, core)

    def share(name, g, dz):
        copy(f"c{name}{g}{dz}", piece(name == "O", dz, (32 * g, 32)), core)

    def mate_step(g):
        wire.arrived(f"m{g}", piece(False, 0, (32 * g, 32)), mate)
        ref = piece(False, 0, part_of("Y", g))
        copy(f"z+Y{g}1", ref, up)
        copy(f"z-Y{g}1", ref, down)
        share("Y", g, 0)

    def left_step(name, g, d):
        same = name == "O"
        part, halves = part_of(name, g), halves_of(name, g)
        for way, sign, dz, to in ((0, "z+", -d, up), (1, "z-", d, down)):
            if d < 4:
                wire.arrived(f"{sign}{name}{g}{d}", piece(same, dz, part), to)
                on = part if d < 3 else halves[way]
                copy(f"{sign}{name}{g}{d + 1}", piece(same, dz, on), to)
            else:
                wire.arrived(f"{sign}{name}{g}{d}", piece(same, dz, halves[way]), to)
        if same:
            for dz in (-d, d)[d // 4:]:
                copy(f"y{g}{dz}", piece(True, dz, late_of(g)), mate)
                share("O", g, dz)

    def late(g, d):
        for dz in (-d, d)[d // 4:]:
            wire.arrived(f"y{g}{dz}", piece(False, dz, late_of(g)), mate)
            share("Y", g, dz)

    def shared(g):
        for name in ("O", "Y"):
            for dz in (0, -1, 1, -2, 2, -3, 3, 4):
                ref = piece(name == "O", dz, (32 * g, 32), 1 - me.e)
                wire.arrived(f"c{name}{g}{dz}", ref, core)

    right_w = jnp.concatenate([rg[...].T, rpw[...].T], axis=0)

    def right_turn():
        @pl.loop(0, 16, unroll=4)
        def _(k):
            first = flat[pl.ds(k, 64, stride=32), :]
            second = flat[pl.ds(k + 16, 64, stride=32), :]
            turned[pl.ds(k, 128, stride=16), :] = gated(
                right_w, jnp.concatenate([first, second], axis=0),
                right_mask(mid_ref, cols_ref, k),
            )

        @pl.loop(0, 16, unroll=4)
        def _(t):
            rows = pl.ds(pl.multiple_of(t * 128, 128), 128)
            part = turned[rows, :].reshape(8, 16, 128).astype(BF)
            rp[me.row, pl.ds(pl.multiple_of(t * 8, 8), 8)] = part

    def right_send(own, g):
        low, high = group_rows(g)
        ref = rp.at[me.across(own, 0)]
        tag = f"{own:d}{g}1"
        copy("x+a" + tag, ref.at[low], east)
        copy("x-b" + tag, ref.at[high], west)
        copy("x+b" + tag, ref.at[high], east)
        copy("x-a" + tag, ref.at[low], west)

    def right_step(own, g):
        low, high = group_rows(g)
        behind, ahead = rp.at[me.across(own, -1), low], rp.at[me.across(own, 1), high]
        wire.arrived(f"x+a{own:d}{g}1", behind, east)
        copy(f"x+a{own:d}{g}2", behind, east)
        wire.arrived(f"x-b{own:d}{g}1", ahead, west)
        copy(f"x-b{own:d}{g}2", ahead, west)

    def right_rest(own, g):
        low, high = group_rows(g)
        behind, ahead = rp.at[me.across(own, -1), high], rp.at[me.across(own, 1), low]
        far = rp.at[me.across(own, 2)]
        wire.arrived(f"x+b{own:d}{g}1", behind, east)
        wire.arrived(f"x-a{own:d}{g}1", ahead, west)
        wire.arrived(f"x+a{own:d}{g}2", far.at[low], east)
        wire.arrived(f"x-b{own:d}{g}2", far.at[high], west)

    def over_y(g):
        low, high = group_rows(g)
        wire.start(f"ya{g}", rp.at[me.row, low], relay.at[0, g], north)
        wire.start(f"yb{g}", rp.at[me.row, high], relay.at[1, g], south)

    def over_y_on(g):
        low, high = group_rows(g)
        here = me.yh * 2 + me.yl
        above, below = lax.rem(here + 3, 4), lax.rem(here + 1, 4)
        wire.arrived(f"ya{g}", relay.at[0, g], north)
        wire.start(f"ya{g}2", relay.at[0, g], rp.at[me.x * 2 + above // 2, low], north)
        wire.arrived(f"yb{g}", relay.at[1, g], south)
        wire.start(f"yb{g}2", relay.at[1, g], rp.at[me.x * 2 + below // 2, high], south)

    def pair_step(g):
        low, high = group_rows(g)
        pair = rp.at[me.across(False, 0)]
        wire.arrived(f"ya{g}2", pair.at[low], north)
        wire.arrived(f"yb{g}2", pair.at[high], south)
        right_send(False, g)

    def keep(g):
        for part in group_rows(g):
            for src, dst in ((lp.at[:, :, part], lp_out.at[:, :, part]),
                             (rp.at[:, part], rp_out.at[:, part])):
                made = pltpu.make_async_copy(src, dst, local.at[len(outs)])
                made.start()
                outs.append(made)

    def triangle(start):
        @pl.loop(0, 16, unroll=8)
        def _(t):
            c = start + t
            right = rp[:, c].reshape(128, 128).T
            right = jnp.concatenate([right[:64], right[64:]], axis=1)
            left = jnp.concatenate(
                [lp[0, :, c].reshape(128, 128), lp[1, :, c].reshape(128, 128)], axis=0
            )
            rows = pl.ds(pl.multiple_of(c * 8, 8), 8)
            tri[:, rows, :] = nn(right, left).reshape(8, 8, 128)

    def keep_triangle(g):
        for part in (pl.ds(256 * g, 256), pl.ds(512 + 256 * g, 256)):
            made = pltpu.make_async_copy(
                tri.at[:, part], tri_out.at[:, part], local.at[len(outs)]
            )
            made.start()
            outs.append(made)

    left_send(0)
    for t in range(4):
        normed_rows(right_ref, t)
    mate_step(0)
    for t in range(4, 8):
        normed_rows(right_ref, t)
    left_step("O", 0, 1)
    right_turn()
    right_send(True, 0)
    over_y(0)
    left_step("Y", 0, 1)
    left_step("O", 0, 2)
    late(0, 1)
    over_y_on(0)
    left_step("Y", 0, 2)
    right_step(True, 0)
    left_step("O", 0, 3)
    late(0, 2)
    pair_step(0)
    right_send(True, 1)
    over_y(1)
    left_step("Y", 0, 3)
    left_send(1)
    left_step("O", 0, 4)
    mate_step(1)
    late(0, 3)
    left_step("Y", 0, 4)
    late(0, 4)
    right_step(False, 0)
    left_step("O", 1, 1)
    over_y_on(1)
    right_rest(True, 0)
    left_step("Y", 1, 1)
    right_rest(False, 0)
    shared(0)
    keep(0)
    left_step("O", 1, 2)
    triangle(0)
    late(1, 1)
    right_step(True, 1)
    left_step("Y", 1, 2)
    triangle(16)
    pair_step(1)
    left_step("O", 1, 3)
    late(1, 2)
    triangle(64)
    left_step("Y", 1, 3)
    triangle(80)
    keep_triangle(0)
    right_step(False, 1)
    left_step("O", 1, 4)
    late(1, 3)
    left_step("Y", 1, 4)
    late(1, 4)
    right_rest(True, 1)
    right_rest(False, 1)
    shared(1)
    keep(1)
    for start in (32, 48, 96, 112):
        triangle(start)
    keep_triangle(1)
    for made in outs:
        made.wait()
    wire.finish()


def gather(*operands):
    return pl.pallas_call(
        gather_kernel,
        out_shape=(
            jax.ShapeDtypeStruct((2, 8, 128, 16, 128), BF),
            jax.ShapeDtypeStruct((8, 128, 16, 128), BF),
            jax.ShapeDtypeStruct((8, 1024, 128), F32),
        ),
        in_specs=[VMEM] * 4 + [SMEM] + [VMEM] * 5,
        out_specs=(ANY, ANY, ANY),
        scratch_shapes=[
            pltpu.VMEM((2, 8, 128, 16, 128), BF),
            pltpu.VMEM((8, 128, 16, 128), BF),
            pltpu.VMEM((8, 1024, 128), F32),
            pltpu.VMEM((2048, 128), F32),
            pltpu.VMEM((2048, 128), F32),
            pltpu.VMEM((1024, 128), F32),
            pltpu.VMEM((512, 128), F32),
            pltpu.VMEM((2, 2, 32, 16, 128), BF),
            pltpu.SemaphoreType.DMA((128,)),
            pltpu.SemaphoreType.DMA((128,)),
            pltpu.SemaphoreType.DMA((12,)),
        ],
        compiler_params=pltpu.CompilerParams(
            collective_id=0, has_side_effects=True, vmem_limit_bytes=LIMIT
        ),
        name="gather_panels",
    )(*operands)


def scatter_kernel(
    lp_hbm, rp_hbm, tri_hbm, left_ref, right_ref, rows_ref, cols_ref, mid_ref, gain_ref,
    lg, lpw, rg, rpw, left_out, right_out,
    lp, rp, tri, dl, dr,
    core_in, z_in, late_in, mate_in, give, got, x_in, relay, pair_in,
    flat_left, flat_right, back, norms, rstds, gates, values,
    send, recv, local,
):
    me = Place()
    wire = Wire(send, recv)
    met = greet(me)
    core, up, down, mate = me.at(e=1), me.at(z=1), me.at(z=-1), me.mate()
    east, west, north, south = me.at(x=1), me.at(x=-1), me.at(y=1), me.at(y=-1)
    gain = gain_ref[...]
    loads = ([], [])

    def load(g, src, dst):
        made = pltpu.make_async_copy(src, dst, local.at[len(loads[0]) + len(loads[1])])
        made.start()
        loads[g].append(made)

    for g in (0, 1):
        for part in group_rows(g):
            rows = pl.ds(part.start * 8, 256)
            load(g, tri_hbm.at[:, rows], tri.at[:, rows])
            load(g, rp_hbm.at[:, part], rp.at[:, part])
            load(g, lp_hbm.at[:, :, part], lp.at[:, :, part])

    fill = Fill()
    left_w = jnp.concatenate([lg[...], lpw[...]], axis=1)
    right_w = jnp.concatenate([rg[...], rpw[...]], axis=1)

    def ahead(ref, t, weights, shift):
        def work():
            _, normed, rstd, gate, value = project(ref, t, gain, weights)
            rows = pl.ds(shift + t * 256, 256)
            norms[rows, :] = normed
            rstds[rows, :] = jnp.broadcast_to(rstd, (256, 128))
            gates[rows, :] = gate
            values[rows, :] = value * gate * (1.0 - gate)

        return work

    for t in range(8):
        fill.todo.append(ahead(right_ref, t, right_w, 1024))
    for t in range(4):
        fill.todo.append(ahead(left_ref, t, left_w, 0))

    def side_back(count, weights, shift, out):
        for t in range(count):
            here, rows = pl.ds(t * 256, 256), pl.ds(shift + t * 256, 256)
            masked = back[here, :]
            d_value = (masked * gates[rows, :]).astype(BF)
            d_gate = (masked * values[rows, :]).astype(BF)
            d_norm = nt(jnp.concatenate([d_gate, d_value], axis=1), weights)
            result = norm_back(norms[rows, :], rstds[rows, :], gain, d_norm, -1)
            out[here, :] = result.astype(BF)

    def panels_back(half, start):
        @pl.loop(0, 16, unroll=8)
        def _(t):
            c = half * 64 + start + t
            rows = pl.ds(pl.multiple_of(c * 8, 8), 8)
            grad = tri[:, rows, :].reshape(64, 128).astype(BF)
            none = jnp.zeros((64, 128), BF)
            grad = jnp.concatenate(
                [
                    jnp.concatenate([grad, none], axis=1),
                    jnp.concatenate([none, grad], axis=1),
                ],
                axis=0,
            )
            right = rp[:, c].reshape(128, 128)
            left = jnp.concatenate(
                [lp[0, :, c].reshape(128, 128), lp[1, :, c].reshape(128, 128)], axis=1
            )
            d_left = nn(right, grad).astype(BF)
            dl[0, :, c] = d_left[:, :128].reshape(8, 16, 128)
            dl[1, :, c] = d_left[:, 128:].reshape(8, 16, 128)
            dr[:, c] = nt(left, grad).astype(BF).reshape(8, 16, 128)

    def block(which, dz, half=None):
        kh, slot = me.slot(which == 1, dz)
        start = (me.e if half is None else half) * 64
        return dl.at[kh, slot, pl.ds(pl.multiple_of(start, 64), 64)]

    def core_send(g):
        part = pl.ds(32 * g, 32)
        for dz in (4, 3, 5, 2, 6, 1, 7, 0):
            for which in (0, 1):
                wire.start(
                    f"c{which}{g}{dz}", block(which, dz, 1 - me.e).at[part],
                    core_in.at[which, dz, part], core,
                )

    def add(target, start, count, terms, out=None):
        def body(t):
            part = pl.ds(pl.multiple_of(start + t * 8, 8), 8)
            total = target[part].astype(F32)
            for term, shift in terms:
                place = pl.ds(pl.multiple_of(start - shift + t * 8, 8), 8)
                total = total + term[place].astype(F32)
            if out is None:
                target[part] = total.astype(BF)
            else:
                out(start // 8 + t, total)

        steps = count // 8
        if steps < 4:
            for t in range(steps):
                body(t)
        else:
            pl.loop(0, steps, unroll=4)(body)

    def ready(which, g, dz):
        part = pl.ds(32 * g, 32)
        wire.arrived(f"c{which}{g}{dz}", core_in.at[which, dz, part], core)
        start, count = late_of(g)
        if which == 0:
            add(block(0, dz), start, count, [(core_in.at[0, dz], 0)])
            wire.start(
                f"l{g}{dz}", block(0, dz).at[pl.ds(start, count)], late_in.at[g, dz], mate
            )
        else:
            wire.arrived(f"l{g}{dz}", late_in.at[g, dz], mate)

    def sum_part(which, g, dz, start, count, more, out=None):
        terms = [(core_in.at[which, dz], 0)] + more
        first, _ = late_of(g)
        plain = min(count, max(0, first - start))
        if plain:
            add(block(which, dz), start, plain, terms, out)
        if which == 1 and start + count > first:
            late = [(late_in.at[g, dz], first)]
            add(block(which, dz), first, start + count - first, terms + late, out)

    def put(name, way, ref, dst, part):
        sign, to = (("+", up), ("-", down))[way]
        wire.start(f"z{sign}{name}", ref.at[pl.ds(*part)], dst.at[pl.ds(*part)], to)

    def came(which, g, way, d):
        name = "O" if which else "Y"
        sign, to = (("+", up), ("-", down))[way]
        part = halves_of(name, g)[way] if d == 0 else part_of(name, g)
        ref = z_in.at[way, which, d]
        wire.arrived(f"z{sign}{name}{g}{d}", ref.at[pl.ds(*part)], to)
        return [(ref, 0)]

    def left_step(which, g, d):
        name = "O" if which else "Y"
        halves = halves_of(name, g)
        if d == 0:
            ready(which, g, 4)
            for way in (0, 1):
                sum_part(which, g, 4, *halves[way], [])
                put(f"{name}{g}0", way, block(which, 4), z_in.at[way, which, 0], halves[way])
            return
        for way in (0, 1):
            dz = 4 + d if way else 4 - d
            ready(which, g, dz)
            more = came(which, g, way, d - 1)
            if d == 1:
                sum_part(which, g, dz, *halves[way], more)
                sum_part(which, g, dz, *halves[1 - way], [])
            else:
                sum_part(which, g, dz, *part_of(name, g), more)
            put(
                f"{name}{g}{d}", way, block(which, dz), z_in.at[way, which, d],
                part_of(name, g),
            )

    def left_last_other(g):
        ready(0, g, 0)
        more = came(0, g, 0, 3) + came(0, g, 1, 3)
        start, count = part_of("Y", g)
        sum_part(0, g, 0, start, count, more)
        wire.start(
            f"mate{g}", block(0, 0).at[pl.ds(start, count)], mate_in.at[g], mate
        )

    def put_left(t, total):
        first, second = total[:, :8].reshape(64, 128), total[:, 8:].reshape(64, 128)
        rows = pl.ds(pl.multiple_of(me.e * 512 + t * 64, 64), 64)
        flat_left[rows, :] = jnp.where(me.e == 0, first, second)
        give[pl.ds(pl.multiple_of(t * 64, 64), 64), :] = jnp.where(me.e == 0, second, first)

    def left_last(g):
        ready(1, g, 0)
        more = came(1, g, 0, 3) + came(1, g, 1, 3)
        wire.arrived(f"mate{g}", mate_in.at[g], mate)
        start, count = part_of("Y", g)
        sum_part(1, g, 0, start, count, more + [(mate_in.at[g], start)], put_left)
        sum_part(1, g, 0, start + count, 8, more, put_left)
        rows = pl.ds(256 * g, 256)
        wire.start(f"last{g}", give.at[rows], got.at[rows], core)

    def column(which, dx):
        return dr.at[me.across(which == 1, dx)]

    def right_first(which, g):
        low, high = group_rows(g)
        ref = column(which, 2)
        wire.start(f"x+{which}{g}0", ref.at[low], x_in.at[0, which, 0, low], east)
        wire.start(f"x-{which}{g}0", ref.at[high], x_in.at[1, which, 0, high], west)

    def right_step(which, g):
        parts = group_rows(g)
        for way, sign, to, dx in ((0, "+", east, 1), (1, "-", west, 3)):
            ref = x_in.at[way, which, 0]
            wire.arrived(f"x{sign}{which}{g}0", ref.at[parts[way]], to)
            add(column(which, dx), parts[way].start, 32, [(ref, 0)])
            for part, tag in zip(parts, "ab"):
                wire.start(
                    f"x{sign}{which}{g}1{tag}", column(which, dx).at[part],
                    x_in.at[way, which, 1, part], to,
                )

    def right_came(which, g):
        for way, sign, to in ((0, "+", east), (1, "-", west)):
            for part, tag in zip(group_rows(g), "ab"):
                ref = x_in.at[way, which, 1, part]
                wire.arrived(f"x{sign}{which}{g}1{tag}", ref, to)
        return [(x_in.at[0, which, 1], 0), (x_in.at[1, which, 1], 0)]

    def right_last_other(g):
        terms = right_came(0, g)
        low, high = group_rows(g)
        for part in (low, high):
            add(column(0, 0), part.start, 32, terms)
        wire.start(f"ya{g}", column(0, 0).at[low], relay.at[0, g], north)
        wire.start(f"yb{g}", column(0, 0).at[high], relay.at[1, g], south)

    def over_y_on(g):
        low, high = group_rows(g)
        wire.arrived(f"ya{g}", relay.at[0, g], north)
        wire.start(f"ya{g}2", relay.at[0, g], pair_in.at[low], north)
        wire.arrived(f"yb{g}", relay.at[1, g], south)
        wire.start(f"yb{g}2", relay.at[1, g], pair_in.at[high], south)

    def put_right(t, total):
        rows = pl.ds(pl.multiple_of(t * 128, 128), 128)
        flat_right[rows, :] = total.reshape(128, 128)

    def right_last(g):
        terms = right_came(1, g)
        low, high = group_rows(g)
        wire.arrived(f"ya{g}2", pair_in.at[low], north)
        wire.arrived(f"yb{g}2", pair_in.at[high], south)
        for part in (low, high):
            add(column(1, 0), part.start, 32, terms + [(pair_in, 0)], put_right)

    for made in loads[0]:
        made.wait()
    for start in (0, 16):
        panels_back(1 - me.e, start)
    met()
    core_send(0)
    for start in (0, 16):
        panels_back(me.e, start)
    right_first(0, 0)
    right_first(1, 0)
    left_step(0, 0, 0)
    left_step(1, 0, 0)
    for made in loads[1]:
        made.wait()
    panels_back(1 - me.e, 32)
    left_step(0, 0, 1)
    right_step(0, 0)
    panels_back(1 - me.e, 48)
    core_send(1)
    left_step(1, 0, 1)
    right_step(1, 0)
    panels_back(me.e, 32)
    left_step(0, 0, 2)
    panels_back(me.e, 48)
    right_first(0, 1)
    right_first(1, 1)
    left_step(1, 0, 2)
    fill(1)
    left_step(0, 0, 3)
    left_step(0, 1, 0)
    right_last_other(0)
    left_step(1, 0, 3)
    left_step(1, 1, 0)
    fill(2)
    right_step(0, 1)
    left_step(0, 1, 1)
    over_y_on(0)
    left_last_other(0)
    left_step(1, 1, 1)
    right_step(1, 1)
    fill(2)
    left_last(0)
    right_last(0)
    fill(1)
    left_step(0, 1, 2)
    fill(2)
    left_step(1, 1, 2)
    right_last_other(1)
    fill(2)
    left_step(0, 1, 3)
    over_y_on(1)
    left_step(1, 1, 3)
    fill(2)
    left_last_other(1)
    right_last(1)

    @pl.loop(0, 16, unroll=4)
    def _(k):
        rows = flat_right[pl.ds(k, 128, stride=16), :] * right_mask(mid_ref, cols_ref, k)
        turned = rows.T
        back[pl.ds(k, 64, stride=32), :] = turned[:64, :]
        back[pl.ds(k + 16, 64, stride=32), :] = turned[64:, :]

    left_last(1)
    side_back(8, right_w, 1024, right_out)
    for g in (0, 1):
        rows = pl.ds(256 * g, 256)
        wire.arrived(f"last{g}", got.at[rows], core)
    flat_left[pl.ds(pl.multiple_of((1 - me.e) * 512, 512), 512), :] = got[...]

    @pl.loop(0, 8, unroll=4)
    def _(k):
        rows = flat_left[pl.ds(k, 128, stride=8), :] * left_mask(mid_ref, rows_ref, k)
        back[pl.ds(k, 128, stride=8), :] = rows.T

    side_back(4, left_w, 0, left_out)
    wire.finish()


def scatter(*operands):
    return pl.pallas_call(
        scatter_kernel,
        out_shape=(
            jax.ShapeDtypeStruct((1024, 128), BF),
            jax.ShapeDtypeStruct((2048, 128), BF),
        ),
        in_specs=[ANY, ANY, ANY] + [VMEM] * 4 + [SMEM] + [VMEM] * 5,
        out_specs=(VMEM, VMEM),
        scratch_shapes=[
            pltpu.VMEM((2, 8, 128, 16, 128), BF),
            pltpu.VMEM((8, 128, 16, 128), BF),
            pltpu.VMEM((8, 1024, 128), F32),
            pltpu.VMEM((2, 8, 128, 16, 128), BF),
            pltpu.VMEM((8, 128, 16, 128), BF),
            pltpu.VMEM((2, 8, 64, 16, 128), BF),
            pltpu.VMEM((2, 2, 4, 64, 16, 128), BF),
            pltpu.VMEM((2, 8, 8, 16, 128), BF),
            pltpu.VMEM((2, 24, 16, 128), BF),
            pltpu.VMEM((512, 128), F32),
            pltpu.VMEM((512, 128), F32),
            pltpu.VMEM((2, 2, 2, 128, 16, 128), BF),
            pltpu.VMEM((2, 2, 32, 16, 128), BF),
            pltpu.VMEM((128, 16, 128), BF),
            pltpu.VMEM((1024, 128), F32),
            pltpu.VMEM((2048, 128), F32),
            pltpu.VMEM((2048, 128), F32),
            pltpu.VMEM((3072, 128), F32),
            pltpu.VMEM((3072, 128), F32),
            pltpu.VMEM((3072, 128), F32),
            pltpu.VMEM((3072, 128), F32),
            pltpu.SemaphoreType.DMA((128,)),
            pltpu.SemaphoreType.DMA((128,)),
            pltpu.SemaphoreType.DMA((12,)),
        ],
        compiler_params=pltpu.CompilerParams(
            collective_id=1, has_side_effects=True, vmem_limit_bytes=LIMIT
        ),
        name="scatter_sums",
    )(*operands)


JS = 8


def middle_kernel(
    tri_ref, tile_ref, up_ref, in_gain_ref, gate_w_ref, mid_gain_ref, proj_w_ref,
    update_ref, d_tile_ref, d_tri_ref, flat,
):
    mid_gain = jnp.broadcast_to(mid_gain_ref[...], (128, 128)).T
    in_gain = in_gain_ref[...]
    proj_w = proj_w_ref[...]
    gate_w = gate_w_ref[...]

    for j in range(JS):
        normed, _ = norm(tri_ref[0, pl.ds(j, 128, stride=8), :], 0)
        value = tn((normed * mid_gain).astype(BF), proj_w)
        flat[pl.ds(j, 128, stride=8), :] = value

    for t in range(8):
        rows = pl.ds(t * 128, 128)
        items = pl.ds(t * 16, 16)
        tile = tile_ref[items].astype(F32).reshape(128, 128)
        upstream = up_ref[items].astype(F32).reshape(128, 128)
        normed, rstd = norm(tile, -1)
        gate = sigmoid(nn((normed * in_gain).astype(BF), gate_w))
        value = flat[rows, :]
        update_ref[items] = (gate * value).reshape(16, 8, 128).astype(BF)
        gated = upstream * gate
        flat[rows, :] = gated
        d_gate = (gated * value * (1.0 - gate)).astype(BF)
        d_norm = nt(d_gate, gate_w)
        d_tile = norm_back(normed, rstd, in_gain, d_norm, -1)
        d_tile_ref[items] = d_tile.reshape(16, 8, 128).astype(BF)

    for j in range(JS):
        here = pl.ds(j, 128, stride=8)
        normed, rstd = norm(tri_ref[0, here, :], 0)
        d_norm = nt(proj_w, flat[here, :].astype(BF))
        d_tri_ref[0, here, :] = norm_back(normed, rstd, mid_gain, d_norm, 0)


def middle(tri, tile, upstream, in_gain, gate_w, mid_gain, proj_w):
    cell = pl.BlockSpec((128, JS, 128), lambda s: (0, s, 0))
    cube = pl.BlockSpec((1, 1024, 128), lambda s: (s, 0, 0))
    whole = pl.BlockSpec((128, 128), lambda s: (0, 0))
    line = pl.BlockSpec((1, 128), lambda s: (0, 0))
    return pl.pallas_call(
        middle_kernel,
        grid=(64 // JS,),
        out_shape=(
            jax.ShapeDtypeStruct((128, 64, 128), BF),
            jax.ShapeDtypeStruct((128, 64, 128), BF),
            jax.ShapeDtypeStruct((8, 1024, 128), F32),
        ),
        in_specs=[cube, cell, cell, line, whole, line, whole],
        out_specs=(cell, cell, cube),
        scratch_shapes=[pltpu.VMEM((1024, 128), F32)],
        compiler_params=pltpu.CompilerParams(
            vmem_limit_bytes=LIMIT, dimension_semantics=("arbitrary",)
        ),
        name="middle",
    )(tri, tile, upstream, in_gain, gate_w, mid_gain, proj_w)


def body(
    pair_left,
    pair_right,
    pair_tile,
    d_update,
    mask_rows,
    mask_cols,
    mask_mid,
    ln_in_gain,
    left_gate_w,
    left_proj_w,
    right_gate_w,
    right_proj_w,
    out_gate_w,
    ln_mid_gain,
    out_proj_w,
):
    flat_left = pair_left.reshape(1024, 128)
    flat_right = pair_right.reshape(2048, 128)
    gain = ln_in_gain.reshape(1, 128)
    sides = (
        flat_left, flat_right, mask_rows.reshape(1, 128), mask_cols.reshape(1, 64),
        mask_mid, gain, left_gate_w, left_proj_w, right_gate_w, right_proj_w,
    )
    lp, rp, tri = gather(*sides)
    update, d_tile, d_tri = middle(
        tri, pair_tile, d_update, gain, out_gate_w, ln_mid_gain.reshape(1, 128), out_proj_w
    )
    d_left, d_right = scatter(lp, rp, d_tri, *sides)
    return (
        update,
        d_left.reshape(128, 8, 128),
        d_right.reshape(64, 32, 128),
        d_tile,
    )


def solution(mesh):
    in_specs = (
        P("row", "col", None),
        P("col", "row", None),
        P("row", "col", None),
        P("row", "col", None),
        P("row"),
        P("col"),
        P(),
        P(),
        P(),
        P(),
        P(),
        P(),
        P(),
        P(),
        P(),
    )
    out_specs = (
        P("row", "col", None),
        P("row", "col", None),
        P("col", "row", None),
        P("row", "col", None),
    )
    return jax.shard_map(body, mesh=mesh, in_specs=in_specs, out_specs=out_specs, check_vma=False)
```

time: 458 us -> 147 us (0.32); the launches traced: 453 us -> 147 us
  waiting for transfers between devices: 300 us -> 0 us
  Pallas kernels: 0 us -> 143 us
  local copies, waits for them, and re-layouts: 63.9 us -> 3.54 us
  matrix products: 53.7 us -> 0 us
  other arithmetic: 21.4 us -> 0 us
  between operations: 14.2 us -> 0.65 us
    reduce_scatter x2 -> x0, waiting for transfers between devices: 169 us -> none  [the longest x1 122 us: body(): lax.psum_scatter(left_full.astype(jnp.bfloat16), 'col', scatter_dimension...]
    pallas_call x0 -> x3, Pallas kernels: none -> 143 us  [the longest x1 64.3 us: gather(): pl.pallas_call(gather_kernel, out_shape=(jax.ShapeDtypeStruct((2, 8, 128,...]
    all_gather x2 -> x0, waiting for transfers between devices: 131 us -> none  [the longest x1 71.5 us: body(): right_panel = lax.all_gather(right, 'row', axis=1, tiled=True)]
    dot_general x15 -> x0, matrix products: 53.7 us -> none  [the longest x1 9.52 us: body(): jnp.einsum('ijc,jkc->kic', d_triangle, right_panel, preferred_element_typ...]
    all_gather x2 -> x0, local copies, waits for them, and re-layouts: 27.4 us -> none  [the longest x1 15.6 us: body(): right_panel = lax.all_gather(right, 'row', axis=1, tiled=True)]
    dot_general x2 -> x0, local copies, waits for them, and re-layouts: 19.6 us -> none  [the longest x1 12.7 us: body(): jnp.einsum('ijc,jkc->kic', d_triangle, right_panel, preferred_element_typ...]
    convert_element_type x7 -> x0, other arithmetic: 13.2 us -> none  [the longest x1 6.94 us: body(): norm_back(tri_normed, tri_rstd, ln_mid_gain, d_tri_norm)]
    unnamed x51 -> x2, local copies, waits for them, and re-layouts: 16.7 us -> 3.54 us
  transfers between devices with their start and end apart: 4 -> 0, of which waited for: 4 -> 0; matrix products, arithmetic and copies ran while one was open for 16% -> 0% of each run, Pallas kernels for 0% -> 0%
where the time goes in v3:
time: 147 us
  Pallas kernels  143 us (97%)
  local copies, waits for them, and re-layouts  3.54 us (2%)
    pallas_call x1, Pallas kernels, gather(): pl.pallas_call(gather_kernel, out_shape=(jax.ShapeDtypeStruct((2, 8, 128,...  64.3 us
    pallas_call x1, Pallas kernels, scatter(): pl.pallas_call(scatter_kernel, out_shape=(jax.ShapeDtypeStruct((1024, 128...  61.9 us
    pallas_call x1, Pallas kernels, middle(): pl.pallas_call(middle_kernel, grid=(64 // JS,), out_shape=(jax.ShapeDtype...  16.8 us
    unnamed x2, local copies, waits for them, and re-layouts  3.54 us

profile of v3, /device:TPU:1, one launch (start us, length us, event | category | flops | bytes accessed | tf_op | source)
XLA Modules:
  0.0 147.2 jit_solution(10553508728072140220)
XLA Ops:
  0.6 64.3 %gather_panels.1 = (bf16[2,8,128,16,128]{4,3,2,1,0:T(8,128)(2,1)}, bf16[8,128,16,128]{3,2,1,0:T(8,128)(2,1)}, f32[8,1024,128]{2,1,0:T(8,128)}) custom-call(bf16[1024,128]{1,0:T(8,128)(2,1)} %bitcast.10, bf16[2048,128]{1,0:T(8,128)(2,1)} %bitcast.8, s32[1,128]{1,0:T(1,128)} %bitcast.17, s32[1,64]{1,0:T(1,128)} %bitcast.19, s32[256]{0:T(256)} %mid_ref.3, ...), custom_call_target="tpu_custom_call" | custom-call | tf_op jit(solution)/shard_map/gather_panels/pallas_call | solution.py:421
  64.9 16.8 %middle.1 = (bf16[128,64,128]{2,1,0:T(8,128)(2,1)}, bf16[128,64,128]{2,1,0:T(8,128)(2,1)}, f32[8,1024,128]{2,1,0:T(8,128)}) custom-call(f32[8,1024,128]{2,1,0:T(8,128)} %get-tuple-element.12.tri_ref, bf16[128,64,128]{2,1,0:T(8,128)(2,1)} %tile_ref.1, bf16[128,64,128]{2,1,0:T(8,128)(2,1)} %up_ref.1, f32[1,128]{1,0:T(1,128)} %bitcast.15, ...), custom_call_target="tpu_custom_call" | custom-call | tf_op jit(solution)/shard_map/middle/pallas_call | solution.py:867
  81.7 61.9 %scatter_sums.1 = (bf16[1024,128]{1,0:T(8,128)(2,1)}, bf16[2048,128]{1,0:T(8,128)(2,1)}) custom-call(bf16[2,8,128,16,128]{4,3,2,1,0:T(8,128)(2,1)} %get-tuple-element.14.lp_hbm, bf16[8,128,16,128]{3,2,1,0:T(8,128)(2,1)} %get-tuple-element.15.rp_hbm, f32[8,1024,128]{2,1,0:T(8,128)} %get-tuple-element.16.tri_hbm, bf16[1024,128]{1,0:T(8,128)(2,1)} %bitcast.11, ...), custom_call_target="tpu_custom_call" | custom-call | tf_op jit(solution)/shard_map/scatter_sums/pallas_call | solution.py:781
  143.6 1.7 %copy.21 = bf16[128,8,128]{2,1,0:T(8,128)(2,1)} copy(bf16[128,8,128]{2,1,0:T(8,128)(2,1)} %bitcast.13) | data formatting | bytes 524288
  145.3 1.9 %copy.22 = bf16[64,32,128]{2,1,0:T(8,128)(2,1)} copy(bf16[64,32,128]{2,1,0:T(8,128)(2,1)} %bitcast.12) | data formatting | bytes 1048576

commit v4 on v3

--- a/solution.py
+++ b/solution.py
@@ -140,21 +140,32 @@
             made.wait_send()
 
 
-def part_of(name, group):
-    return (32 * group, 32 if name == "O" else 24)
-
-
-def late_of(group):
-    return (32 * group + 24, 8)
-
-
-def halves_of(name, group):
-    start, count = part_of(name, group)
-    return (start, 16), (start + 16, count - 16)
-
-
-def group_rows(group):
-    return pl.ds(32 * group, 32), pl.ds(64 + 32 * group, 32)
+class Groups:
+    def __init__(self, *sizes):
+        self.size = sizes
+        self.start = tuple(sum(sizes[:g]) for g in range(len(sizes)))
+
+    def whole(self, g):
+        return (self.start[g], self.size[g])
+
+    def part(self, name, g):
+        return (self.start[g], self.size[g] - (0 if name == "O" else 8))
+
+    def late(self, g):
+        return (self.start[g] + self.size[g] - 8, 8)
+
+    def halves(self, name, g):
+        start, count = self.part(name, g)
+        first = count - 16 if name == "O" else count // 2
+        return (start, first), (start + first, count - first)
+
+    def rows(self, g):
+        start, size = self.whole(g)
+        return pl.ds(start, size), pl.ds(64 + start, size)
+
+
+FORTH = Groups(40, 24)
+BACK = Groups(24, 40)
 
 
 def gather_kernel(
@@ -199,6 +210,8 @@
     met()
     there = pl.ds(pl.multiple_of((1 - me.e) * 512, 512), 512)
     wire.start("core", turned_left.at[there], given, core)
+    for t in range(4):
+        normed_rows(right_ref, t)
     wire.arrived("core", given, core)
     own_kh, own_slot = me.slot(True, 0)
 
@@ -216,25 +229,25 @@
         wire.start(name, ref, ref, to)
 
     def left_send(g):
-        ref = piece(True, 0, part_of("O", g))
+        ref = piece(True, 0, FORTH.part("O", g))
         copy(f"z+O{g}1", ref, up)
         copy(f"z-O{g}1", ref, down)
         copy(f"m{g}", ref, mate)
         copy(f"cO{g}0", ref, core)
 
     def share(name, g, dz):
-        copy(f"c{name}{g}{dz}", piece(name == "O", dz, (32 * g, 32)), core)
+        copy(f"c{name}{g}{dz}", piece(name == "O", dz, FORTH.whole(g)), core)
 
     def mate_step(g):
-        wire.arrived(f"m{g}", piece(False, 0, (32 * g, 32)), mate)
-        ref = piece(False, 0, part_of("Y", g))
+        wire.arrived(f"m{g}", piece(False, 0, FORTH.whole(g)), mate)
+        ref = piece(False, 0, FORTH.part("Y", g))
         copy(f"z+Y{g}1", ref, up)
         copy(f"z-Y{g}1", ref, down)
         share("Y", g, 0)
 
     def left_step(name, g, d):
         same = name == "O"
-        part, halves = part_of(name, g), halves_of(name, g)
+        part, halves = FORTH.part(name, g), FORTH.halves(name, g)
         for way, sign, dz, to in ((0, "z+", -d, up), (1, "z-", d, down)):
             if d < 4:
                 wire.arrived(f"{sign}{name}{g}{d}", piece(same, dz, part), to)
@@ -244,18 +257,18 @@
                 wire.arrived(f"{sign}{name}{g}{d}", piece(same, dz, halves[way]), to)
         if same:
             for dz in (-d, d)[d // 4:]:
-                copy(f"y{g}{dz}", piece(True, dz, late_of(g)), mate)
+                copy(f"y{g}{dz}", piece(True, dz, FORTH.late(g)), mate)
                 share("O", g, dz)
 
     def late(g, d):
         for dz in (-d, d)[d // 4:]:
-            wire.arrived(f"y{g}{dz}", piece(False, dz, late_of(g)), mate)
+            wire.arrived(f"y{g}{dz}", piece(False, dz, FORTH.late(g)), mate)
             share("Y", g, dz)
 
     def shared(g):
         for name in ("O", "Y"):
             for dz in (0, -1, 1, -2, 2, -3, 3, 4):
-                ref = piece(name == "O", dz, (32 * g, 32), 1 - me.e)
+                ref = piece(name == "O", dz, FORTH.whole(g), 1 - me.e)
                 wire.arrived(f"c{name}{g}{dz}", ref, core)
 
     right_w = jnp.concatenate([rg[...].T, rpw[...].T], axis=0)
@@ -277,7 +290,7 @@
             rp[me.row, pl.ds(pl.multiple_of(t * 8, 8), 8)] = part
 
     def right_send(own, g):
-        low, high = group_rows(g)
+        low, high = FORTH.rows(g)
         ref = rp.at[me.across(own, 0)]
         tag = f"{own:d}{g}1"
         copy("x+a" + tag, ref.at[low], east)
@@ -286,7 +299,7 @@
         copy("x-a" + tag, ref.at[low], west)
 
     def right_step(own, g):
-        low, high = group_rows(g)
+        low, high = FORTH.rows(g)
         behind, ahead = rp.at[me.across(own, -1), low], rp.at[me.across(own, 1), high]
         wire.arrived(f"x+a{own:d}{g}1", behind, east)
         copy(f"x+a{own:d}{g}2", behind, east)
@@ -294,7 +307,7 @@
         copy(f"x-b{own:d}{g}2", ahead, west)
 
     def right_rest(own, g):
-        low, high = group_rows(g)
+        low, high = FORTH.rows(g)
         behind, ahead = rp.at[me.across(own, -1), high], rp.at[me.across(own, 1), low]
         far = rp.at[me.across(own, 2)]
         wire.arrived(f"x+b{own:d}{g}1", behind, east)
@@ -303,36 +316,36 @@
         wire.arrived(f"x-b{own:d}{g}2", far.at[high], west)
 
     def over_y(g):
-        low, high = group_rows(g)
-        wire.start(f"ya{g}", rp.at[me.row, low], relay.at[0, g], north)
-        wire.start(f"yb{g}", rp.at[me.row, high], relay.at[1, g], south)
+        low, high = FORTH.rows(g)
+        wire.start(f"ya{g}", rp.at[me.row, low], relay.at[0, g, pl.ds(0, FORTH.size[g])], north)
+        wire.start(f"yb{g}", rp.at[me.row, high], relay.at[1, g, pl.ds(0, FORTH.size[g])], south)
 
     def over_y_on(g):
-        low, high = group_rows(g)
+        low, high = FORTH.rows(g)
         here = me.yh * 2 + me.yl
         above, below = lax.rem(here + 3, 4), lax.rem(here + 1, 4)
-        wire.arrived(f"ya{g}", relay.at[0, g], north)
-        wire.start(f"ya{g}2", relay.at[0, g], rp.at[me.x * 2 + above // 2, low], north)
-        wire.arrived(f"yb{g}", relay.at[1, g], south)
-        wire.start(f"yb{g}2", relay.at[1, g], rp.at[me.x * 2 + below // 2, high], south)
+        wire.arrived(f"ya{g}", relay.at[0, g, pl.ds(0, FORTH.size[g])], north)
+        wire.start(f"ya{g}2", relay.at[0, g, pl.ds(0, FORTH.size[g])], rp.at[me.x * 2 + above // 2, low], north)
+        wire.arrived(f"yb{g}", relay.at[1, g, pl.ds(0, FORTH.size[g])], south)
+        wire.start(f"yb{g}2", relay.at[1, g, pl.ds(0, FORTH.size[g])], rp.at[me.x * 2 + below // 2, high], south)
 
     def pair_step(g):
-        low, high = group_rows(g)
+        low, high = FORTH.rows(g)
         pair = rp.at[me.across(False, 0)]
         wire.arrived(f"ya{g}2", pair.at[low], north)
         wire.arrived(f"yb{g}2", pair.at[high], south)
         right_send(False, g)
 
     def keep(g):
-        for part in group_rows(g):
+        for part in FORTH.rows(g):
             for src, dst in ((lp.at[:, :, part], lp_out.at[:, :, part]),
                              (rp.at[:, part], rp_out.at[:, part])):
                 made = pltpu.make_async_copy(src, dst, local.at[len(outs)])
                 made.start()
                 outs.append(made)
 
-    def triangle(start):
-        @pl.loop(0, 16, unroll=8)
+    def triangle(start, count):
+        @pl.loop(0, count, unroll=8)
         def _(t):
             c = start + t
             right = rp[:, c].reshape(128, 128).T
@@ -344,7 +357,8 @@
             tri[:, rows, :] = nn(right, left).reshape(8, 8, 128)
 
     def keep_triangle(g):
-        for part in (pl.ds(256 * g, 256), pl.ds(512 + 256 * g, 256)):
+        for rows in FORTH.rows(g):
+            part = pl.ds(rows.start * 8, rows.size * 8)
             made = pltpu.make_async_copy(
                 tri.at[:, part], tri_out.at[:, part], local.at[len(outs)]
             )
@@ -352,65 +366,63 @@
             outs.append(made)
 
     left_send(0)
-    for t in range(4):
-        normed_rows(right_ref, t)
-    mate_step(0)
+    left_send(1)
     for t in range(4, 8):
         normed_rows(right_ref, t)
-    left_step("O", 0, 1)
     right_turn()
     right_send(True, 0)
     over_y(0)
+    mate_step(0)
+    left_step("O", 0, 1)
     left_step("Y", 0, 1)
     left_step("O", 0, 2)
     late(0, 1)
     over_y_on(0)
     left_step("Y", 0, 2)
     right_step(True, 0)
+    right_send(True, 1)
+    mate_step(1)
     left_step("O", 0, 3)
     late(0, 2)
     pair_step(0)
-    right_send(True, 1)
     over_y(1)
     left_step("Y", 0, 3)
-    left_send(1)
+    left_step("O", 1, 1)
     left_step("O", 0, 4)
-    mate_step(1)
     late(0, 3)
     left_step("Y", 0, 4)
+    left_step("Y", 1, 1)
     late(0, 4)
     right_step(False, 0)
-    left_step("O", 1, 1)
     over_y_on(1)
+    left_step("O", 1, 2)
     right_rest(True, 0)
-    left_step("Y", 1, 1)
+    late(1, 1)
+    right_step(True, 1)
+    left_step("Y", 1, 2)
     right_rest(False, 0)
     shared(0)
     keep(0)
-    left_step("O", 1, 2)
-    triangle(0)
-    late(1, 1)
-    right_step(True, 1)
-    left_step("Y", 1, 2)
-    triangle(16)
+    triangle(0, 16)
+    left_step("O", 1, 3)
     pair_step(1)
-    left_step("O", 1, 3)
+    triangle(16, 24)
     late(1, 2)
-    triangle(64)
     left_step("Y", 1, 3)
-    triangle(80)
-    keep_triangle(0)
-    right_step(False, 1)
+    triangle(64, 16)
     left_step("O", 1, 4)
     late(1, 3)
+    right_step(False, 1)
+    triangle(80, 24)
+    keep_triangle(0)
     left_step("Y", 1, 4)
     late(1, 4)
     right_rest(True, 1)
     right_rest(False, 1)
     shared(1)
     keep(1)
-    for start in (32, 48, 96, 112):
-        triangle(start)
+    triangle(40, 24)
+    triangle(104, 24)
     keep_triangle(1)
     for made in outs:
         made.wait()
@@ -435,7 +447,7 @@
             pltpu.VMEM((2048, 128), F32),
             pltpu.VMEM((1024, 128), F32),
             pltpu.VMEM((512, 128), F32),
-            pltpu.VMEM((2, 2, 32, 16, 128), BF),
+            pltpu.VMEM((2, 2, 40, 16, 128), BF),
             pltpu.SemaphoreType.DMA((128,)),
             pltpu.SemaphoreType.DMA((128,)),
             pltpu.SemaphoreType.DMA((12,)),
@@ -449,7 +461,7 @@
 
 def scatter_kernel(
     lp_hbm, rp_hbm, tri_hbm, left_ref, right_ref, rows_ref, cols_ref, mid_ref, gain_ref,
-    lg, lpw, rg, rpw, left_out, right_out,
+    lg, lpw, rg, rpw, both_out,
     lp, rp, tri, dl, dr,
     core_in, z_in, late_in, mate_in, give, got, x_in, relay, pair_in,
     flat_left, flat_right, back, norms, rstds, gates, values,
@@ -469,8 +481,8 @@
         loads[g].append(made)
 
     for g in (0, 1):
-        for part in group_rows(g):
-            rows = pl.ds(part.start * 8, 256)
+        for part in BACK.rows(g):
+            rows = pl.ds(part.start * 8, part.size * 8)
             load(g, tri_hbm.at[:, rows], tri.at[:, rows])
             load(g, rp_hbm.at[:, part], rp.at[:, part])
             load(g, lp_hbm.at[:, :, part], lp.at[:, :, part])
@@ -495,18 +507,18 @@
     for t in range(4):
         fill.todo.append(ahead(left_ref, t, left_w, 0))
 
-    def side_back(count, weights, shift, out):
-        for t in range(count):
+    def side_back(steps, weights, shift):
+        for t in steps:
             here, rows = pl.ds(t * 256, 256), pl.ds(shift + t * 256, 256)
             masked = back[here, :]
             d_value = (masked * gates[rows, :]).astype(BF)
             d_gate = (masked * values[rows, :]).astype(BF)
             d_norm = nt(jnp.concatenate([d_gate, d_value], axis=1), weights)
             result = norm_back(norms[rows, :], rstds[rows, :], gain, d_norm, -1)
-            out[here, :] = result.astype(BF)
-
-    def panels_back(half, start):
-        @pl.loop(0, 16, unroll=8)
+            both_out[rows, :] = result.astype(BF)
+
+    def panels_back(half, start, count):
+        @pl.loop(0, count, unroll=8)
         def _(t):
             c = half * 64 + start + t
             rows = pl.ds(pl.multiple_of(c * 8, 8), 8)
@@ -534,7 +546,7 @@
         return dl.at[kh, slot, pl.ds(pl.multiple_of(start, 64), 64)]
 
     def core_send(g):
-        part = pl.ds(32 * g, 32)
+        part = pl.ds(*BACK.whole(g))
         for dz in (4, 3, 5, 2, 6, 1, 7, 0):
             for which in (0, 1):
                 wire.start(
@@ -555,16 +567,16 @@
                 out(start // 8 + t, total)
 
         steps = count // 8
-        if steps < 4:
+        if steps < 6:
             for t in range(steps):
                 body(t)
         else:
             pl.loop(0, steps, unroll=4)(body)
 
     def ready(which, g, dz):
-        part = pl.ds(32 * g, 32)
+        part = pl.ds(*BACK.whole(g))
         wire.arrived(f"c{which}{g}{dz}", core_in.at[which, dz, part], core)
-        start, count = late_of(g)
+        start, count = BACK.late(g)
         if which == 0:
             add(block(0, dz), start, count, [(core_in.at[0, dz], 0)])
             wire.start(
@@ -575,7 +587,7 @@
 
     def sum_part(which, g, dz, start, count, more, out=None):
         terms = [(core_in.at[which, dz], 0)] + more
-        first, _ = late_of(g)
+        first, _ = BACK.late(g)
         plain = min(count, max(0, first - start))
         if plain:
             add(block(which, dz), start, plain, terms, out)
@@ -590,14 +602,14 @@
     def came(which, g, way, d):
         name = "O" if which else "Y"
         sign, to = (("+", up), ("-", down))[way]
-        part = halves_of(name, g)[way] if d == 0 else part_of(name, g)
+        part = BACK.halves(name, g)[way] if d == 0 else BACK.part(name, g)
         ref = z_in.at[way, which, d]
         wire.arrived(f"z{sign}{name}{g}{d}", ref.at[pl.ds(*part)], to)
         return [(ref, 0)]
 
     def left_step(which, g, d):
         name = "O" if which else "Y"
-        halves = halves_of(name, g)
+        halves = BACK.halves(name, g)
         if d == 0:
             ready(which, g, 4)
             for way in (0, 1):
@@ -612,19 +624,20 @@
                 sum_part(which, g, dz, *halves[way], more)
                 sum_part(which, g, dz, *halves[1 - way], [])
             else:
-                sum_part(which, g, dz, *part_of(name, g), more)
+                sum_part(which, g, dz, *BACK.part(name, g), more)
             put(
                 f"{name}{g}{d}", way, block(which, dz), z_in.at[way, which, d],
-                part_of(name, g),
+                BACK.part(name, g),
             )
 
     def left_last_other(g):
         ready(0, g, 0)
         more = came(0, g, 0, 3) + came(0, g, 1, 3)
-        start, count = part_of("Y", g)
+        start, count = BACK.part("Y", g)
         sum_part(0, g, 0, start, count, more)
         wire.start(
-            f"mate{g}", block(0, 0).at[pl.ds(start, count)], mate_in.at[g], mate
+            f"mate{g}", block(0, 0).at[pl.ds(start, count)],
+            mate_in.at[g, pl.ds(0, count)], mate,
         )
 
     def put_left(t, total):
@@ -636,28 +649,28 @@
     def left_last(g):
         ready(1, g, 0)
         more = came(1, g, 0, 3) + came(1, g, 1, 3)
-        wire.arrived(f"mate{g}", mate_in.at[g], mate)
-        start, count = part_of("Y", g)
+        start, count = BACK.part("Y", g)
+        wire.arrived(f"mate{g}", mate_in.at[g, pl.ds(0, count)], mate)
         sum_part(1, g, 0, start, count, more + [(mate_in.at[g], start)], put_left)
         sum_part(1, g, 0, start + count, 8, more, put_left)
-        rows = pl.ds(256 * g, 256)
+        rows = pl.ds(BACK.start[g] * 8, BACK.size[g] * 8)
         wire.start(f"last{g}", give.at[rows], got.at[rows], core)
 
     def column(which, dx):
         return dr.at[me.across(which == 1, dx)]
 
     def right_first(which, g):
-        low, high = group_rows(g)
+        low, high = BACK.rows(g)
         ref = column(which, 2)
         wire.start(f"x+{which}{g}0", ref.at[low], x_in.at[0, which, 0, low], east)
         wire.start(f"x-{which}{g}0", ref.at[high], x_in.at[1, which, 0, high], west)
 
     def right_step(which, g):
-        parts = group_rows(g)
+        parts = BACK.rows(g)
         for way, sign, to, dx in ((0, "+", east, 1), (1, "-", west, 3)):
             ref = x_in.at[way, which, 0]
             wire.arrived(f"x{sign}{which}{g}0", ref.at[parts[way]], to)
-            add(column(which, dx), parts[way].start, 32, [(ref, 0)])
+            add(column(which, dx), parts[way].start, BACK.size[g], [(ref, 0)])
             for part, tag in zip(parts, "ab"):
                 wire.start(
                     f"x{sign}{which}{g}1{tag}", column(which, dx).at[part],
@@ -666,25 +679,25 @@
 
     def right_came(which, g):
         for way, sign, to in ((0, "+", east), (1, "-", west)):
-            for part, tag in zip(group_rows(g), "ab"):
+            for part, tag in zip(BACK.rows(g), "ab"):
                 ref = x_in.at[way, which, 1, part]
                 wire.arrived(f"x{sign}{which}{g}1{tag}", ref, to)
         return [(x_in.at[0, which, 1], 0), (x_in.at[1, which, 1], 0)]
 
     def right_last_other(g):
         terms = right_came(0, g)
-        low, high = group_rows(g)
+        low, high = BACK.rows(g)
         for part in (low, high):
-            add(column(0, 0), part.start, 32, terms)
-        wire.start(f"ya{g}", column(0, 0).at[low], relay.at[0, g], north)
-        wire.start(f"yb{g}", column(0, 0).at[high], relay.at[1, g], south)
+            add(column(0, 0), part.start, BACK.size[g], terms)
+        wire.start(f"ya{g}", column(0, 0).at[low], relay.at[0, g, pl.ds(0, BACK.size[g])], north)
+        wire.start(f"yb{g}", column(0, 0).at[high], relay.at[1, g, pl.ds(0, BACK.size[g])], south)
 
     def over_y_on(g):
-        low, high = group_rows(g)
-        wire.arrived(f"ya{g}", relay.at[0, g], north)
-        wire.start(f"ya{g}2", relay.at[0, g], pair_in.at[low], north)
-        wire.arrived(f"yb{g}", relay.at[1, g], south)
-        wire.start(f"yb{g}2", relay.at[1, g], pair_in.at[high], south)
+        low, high = BACK.rows(g)
+        wire.arrived(f"ya{g}", relay.at[0, g, pl.ds(0, BACK.size[g])], north)
+        wire.start(f"ya{g}2", relay.at[0, g, pl.ds(0, BACK.size[g])], pair_in.at[low], north)
+        wire.arrived(f"yb{g}", relay.at[1, g, pl.ds(0, BACK.size[g])], south)
+        wire.start(f"yb{g}2", relay.at[1, g, pl.ds(0, BACK.size[g])], pair_in.at[high], south)
 
     def put_right(t, total):
         rows = pl.ds(pl.multiple_of(t * 128, 128), 128)
@@ -692,45 +705,43 @@
 
     def right_last(g):
         terms = right_came(1, g)
-        low, high = group_rows(g)
+        low, high = BACK.rows(g)
         wire.arrived(f"ya{g}2", pair_in.at[low], north)
         wire.arrived(f"yb{g}2", pair_in.at[high], south)
         for part in (low, high):
-            add(column(1, 0), part.start, 32, terms + [(pair_in, 0)], put_right)
+            add(column(1, 0), part.start, BACK.size[g], terms + [(pair_in, 0)], put_right)
 
     for made in loads[0]:
         made.wait()
-    for start in (0, 16):
-        panels_back(1 - me.e, start)
+    panels_back(1 - me.e, 0, 24)
     met()
     core_send(0)
-    for start in (0, 16):
-        panels_back(me.e, start)
+    panels_back(me.e, 0, 24)
     right_first(0, 0)
     right_first(1, 0)
     left_step(0, 0, 0)
     left_step(1, 0, 0)
     for made in loads[1]:
         made.wait()
-    panels_back(1 - me.e, 32)
+    panels_back(1 - me.e, 24, 16)
     left_step(0, 0, 1)
     right_step(0, 0)
-    panels_back(1 - me.e, 48)
+    panels_back(1 - me.e, 40, 24)
     core_send(1)
     left_step(1, 0, 1)
     right_step(1, 0)
-    panels_back(me.e, 32)
+    panels_back(me.e, 24, 16)
     left_step(0, 0, 2)
-    panels_back(me.e, 48)
+    panels_back(me.e, 40, 24)
     right_first(0, 1)
     right_first(1, 1)
     left_step(1, 0, 2)
+    left_step(0, 1, 0)
+    left_step(1, 1, 0)
     fill(1)
     left_step(0, 0, 3)
-    left_step(0, 1, 0)
     right_last_other(0)
     left_step(1, 0, 3)
-    left_step(1, 1, 0)
     fill(2)
     right_step(0, 1)
     left_step(0, 1, 1)
@@ -738,7 +749,7 @@
     left_last_other(0)
     left_step(1, 1, 1)
     right_step(1, 1)
-    fill(2)
+    fill(3)
     left_last(0)
     right_last(0)
     fill(1)
@@ -746,12 +757,10 @@
     fill(2)
     left_step(1, 1, 2)
     right_last_other(1)
-    fill(2)
+    fill(3)
     left_step(0, 1, 3)
     over_y_on(1)
     left_step(1, 1, 3)
-    fill(2)
-    left_last_other(1)
     right_last(1)
 
     @pl.loop(0, 16, unroll=4)
@@ -761,10 +770,12 @@
         back[pl.ds(k, 64, stride=32), :] = turned[:64, :]
         back[pl.ds(k + 16, 64, stride=32), :] = turned[64:, :]
 
+    left_last_other(1)
+    side_back(range(5), right_w, 1024)
     left_last(1)
-    side_back(8, right_w, 1024, right_out)
+    side_back(range(5, 8), right_w, 1024)
     for g in (0, 1):
-        rows = pl.ds(256 * g, 256)
+        rows = pl.ds(BACK.start[g] * 8, BACK.size[g] * 8)
         wire.arrived(f"last{g}", got.at[rows], core)
     flat_left[pl.ds(pl.multiple_of((1 - me.e) * 512, 512), 512), :] = got[...]
 
@@ -773,19 +784,16 @@
         rows = flat_left[pl.ds(k, 128, stride=8), :] * left_mask(mid_ref, rows_ref, k)
         back[pl.ds(k, 128, stride=8), :] = rows.T
 
-    side_back(4, left_w, 0, left_out)
+    side_back(range(4), left_w, 0)
     wire.finish()
 
 
 def scatter(*operands):
     return pl.pallas_call(
         scatter_kernel,
-        out_shape=(
-            jax.ShapeDtypeStruct((1024, 128), BF),
-            jax.ShapeDtypeStruct((2048, 128), BF),
-        ),
+        out_shape=jax.ShapeDtypeStruct((3072, 128), BF),
         in_specs=[ANY, ANY, ANY] + [VMEM] * 4 + [SMEM] + [VMEM] * 5,
-        out_specs=(VMEM, VMEM),
+        out_specs=VMEM,
         scratch_shapes=[
             pltpu.VMEM((2, 8, 128, 16, 128), BF),
             pltpu.VMEM((8, 128, 16, 128), BF),
@@ -795,11 +803,11 @@
             pltpu.VMEM((2, 8, 64, 16, 128), BF),
             pltpu.VMEM((2, 2, 4, 64, 16, 128), BF),
             pltpu.VMEM((2, 8, 8, 16, 128), BF),
-            pltpu.VMEM((2, 24, 16, 128), BF),
+            pltpu.VMEM((2, 32, 16, 128), BF),
             pltpu.VMEM((512, 128), F32),
             pltpu.VMEM((512, 128), F32),
             pltpu.VMEM((2, 2, 2, 128, 16, 128), BF),
-            pltpu.VMEM((2, 2, 32, 16, 128), BF),
+            pltpu.VMEM((2, 2, 40, 16, 128), BF),
             pltpu.VMEM((128, 16, 128), BF),
             pltpu.VMEM((1024, 128), F32),
             pltpu.VMEM((2048, 128), F32),
@@ -819,12 +827,39 @@
     )(*operands)
 
 
+def split_kernel(both, left_out, right_out, local):
+    made = []
+    for step in range(6):
+        src = both.at[pl.ds(step * 512, 512)]
+        out, shift = (left_out, 0) if step < 2 else (right_out, 2)
+        dst = out.at[pl.ds((step - shift) * 512, 512)]
+        made.append(pltpu.make_async_copy(src, dst, local.at[step]))
+    for one in made:
+        one.start()
+    for one in made:
+        one.wait()
+
+
+def split(both):
+    return pl.pallas_call(
+        split_kernel,
+        out_shape=(
+            jax.ShapeDtypeStruct((1024, 128), BF),
+            jax.ShapeDtypeStruct((2048, 128), BF),
+        ),
+        in_specs=[ANY],
+        out_specs=(ANY, ANY),
+        scratch_shapes=[pltpu.SemaphoreType.DMA((6,))],
+        name="split_sides",
+    )(both)
+
+
 JS = 8
 
 
 def middle_kernel(
     tri_ref, tile_ref, up_ref, in_gain_ref, gate_w_ref, mid_gain_ref, proj_w_ref,
-    update_ref, d_tile_ref, d_tri_ref, flat,
+    update_ref, d_tile_ref, d_tri_ref, flat, rstds,
 ):
     mid_gain = jnp.broadcast_to(mid_gain_ref[...], (128, 128)).T
     in_gain = in_gain_ref[...]
@@ -832,7 +867,9 @@
     gate_w = gate_w_ref[...]
 
     for j in range(JS):
-        normed, _ = norm(tri_ref[0, pl.ds(j, 128, stride=8), :], 0)
+        normed, rstd = norm(tri_ref[0, pl.ds(j, 128, stride=8), :], 0)
+        d_tri_ref[0, pl.ds(j, 128, stride=8), :] = normed
+        rstds[pl.ds(j, 1), :] = rstd
         value = tn((normed * mid_gain).astype(BF), proj_w)
         flat[pl.ds(j, 128, stride=8), :] = value
 
@@ -854,7 +891,7 @@
 
     for j in range(JS):
         here = pl.ds(j, 128, stride=8)
-        normed, rstd = norm(tri_ref[0, here, :], 0)
+        normed, rstd = d_tri_ref[0, here, :], rstds[pl.ds(j, 1), :]
         d_norm = nt(proj_w, flat[here, :].astype(BF))
         d_tri_ref[0, here, :] = norm_back(normed, rstd, mid_gain, d_norm, 0)
 
@@ -874,7 +911,7 @@
         ),
         in_specs=[cube, cell, cell, line, whole, line, whole],
         out_specs=(cell, cell, cube),
-        scratch_shapes=[pltpu.VMEM((1024, 128), F32)],
+        scratch_shapes=[pltpu.VMEM((1024, 128), F32), pltpu.VMEM((JS, 128), F32)],
         compiler_params=pltpu.CompilerParams(
             vmem_limit_bytes=LIMIT, dimension_semantics=("arbitrary",)
         ),
@@ -910,7 +947,7 @@
     update, d_tile, d_tri = middle(
         tri, pair_tile, d_update, gain, out_gate_w, ln_mid_gain.reshape(1, 128), out_proj_w
     )
-    d_left, d_right = scatter(lp, rp, d_tri, *sides)
+    d_left, d_right = split(scatter(lp, rp, d_tri, *sides))
     return (
         update,
         d_left.reshape(128, 8, 128),

time: 147 us -> 168 us (1.14)
  Pallas kernels: 143 us -> 167 us
  local copies, waits for them, and re-layouts: 3.54 us -> 0 us
    pallas_call x1 -> x2, Pallas kernels: 61.9 us -> 86.2 us  [the longest x1 61.2 us: scatter(): pl.pallas_call(scatter_kernel, out_shape=jax.ShapeDtypeStruct((3072, 128)...]
    unnamed x2 -> x0, local copies, waits for them, and re-layouts: 3.54 us -> none
where the time goes in v4:
time: 168 us
  Pallas kernels  167 us (99%)
    pallas_call x1, Pallas kernels, gather(): pl.pallas_call(gather_kernel, out_shape=(jax.ShapeDtypeStruct((2, 8, 128,...  63.9 us
    pallas_call x1, Pallas kernels, scatter(): pl.pallas_call(scatter_kernel, out_shape=jax.ShapeDtypeStruct((3072, 128)...  61.2 us
    pallas_call x1, Pallas kernels, split(): pl.pallas_call(split_kernel, out_shape=(jax.ShapeDtypeStruct((1024, 128),...  25 us
    pallas_call x1, Pallas kernels, middle(): pl.pallas_call(middle_kernel, grid=(64 // JS,), out_shape=(jax.ShapeDtype...  16.9 us

profile of v4, /device:TPU:1, one launch (start us, length us, event | category | flops | bytes accessed | tf_op | source)
XLA Modules:
  0.0 167.7 jit_solution(3021862689357658604)
XLA Ops:
  0.6 63.9 %gather_panels.1 = (bf16[2,8,128,16,128]{4,3,2,1,0:T(8,128)(2,1)}, bf16[8,128,16,128]{3,2,1,0:T(8,128)(2,1)}, f32[8,1024,128]{2,1,0:T(8,128)}) custom-call(bf16[1024,128]{1,0:T(8,128)(2,1)} %bitcast.10, bf16[2048,128]{1,0:T(8,128)(2,1)} %bitcast.8, s32[1,128]{1,0:T(1,128)} %bitcast.15, s32[1,64]{1,0:T(1,128)} %bitcast.17, s32[256]{0:T(256)} %mid_ref.3, ...), custom_call_target="tpu_custom_call" | custom-call | tf_op jit(solution)/shard_map/gather_panels/pallas_call | solution.py:433
  64.6 16.9 %middle.1 = (bf16[128,64,128]{2,1,0:T(8,128)(2,1)}, bf16[128,64,128]{2,1,0:T(8,128)(2,1)}, f32[8,1024,128]{2,1,0:T(8,128)}) custom-call(f32[8,1024,128]{2,1,0:T(8,128)} %get-tuple-element.12.tri_ref, bf16[128,64,128]{2,1,0:T(8,128)(2,1)} %tile_ref.1, bf16[128,64,128]{2,1,0:T(8,128)(2,1)} %up_ref.1, f32[1,128]{1,0:T(1,128)} %bitcast.13, ...), custom_call_target="tpu_custom_call" | custom-call | tf_op jit(solution)/shard_map/middle/pallas_call | solution.py:904
  81.4 61.2 %scatter_sums.1.both = bf16[3072,128]{1,0:T(8,128)(2,1)} custom-call(bf16[2,8,128,16,128]{4,3,2,1,0:T(8,128)(2,1)} %get-tuple-element.14.lp_hbm, bf16[8,128,16,128]{3,2,1,0:T(8,128)(2,1)} %get-tuple-element.15.rp_hbm, f32[8,1024,128]{2,1,0:T(8,128)} %get-tuple-element.16.tri_hbm, bf16[1024,128]{1,0:T(8,128)(2,1)} %bitcast.11, bf16[2048,128]{1,0:T(8,128)(2,1)} %bitcast.9, ...), custom_call_target="tpu_custom_call" | custom-call | tf_op jit(solution)/shard_map/scatter_sums/pallas_call | solution.py:792
  142.6 25.0 %split_sides.1 = (bf16[1024,128]{1,0:T(8,128)(2,1)}, bf16[2048,128]{1,0:T(8,128)(2,1)}) custom-call(bf16[3072,128]{1,0:T(8,128)(2,1)} %scatter_sums.1.both), custom_call_target="tpu_custom_call" | custom-call | tf_op jit(solution)/shard_map/split_sides/pallas_call | solution.py:844

commit v5 on v4

--- a/solution.py
+++ b/solution.py
@@ -378,45 +378,45 @@
     left_step("O", 0, 2)
     late(0, 1)
     over_y_on(0)
+    mate_step(1)
+    left_step("O", 1, 1)
     left_step("Y", 0, 2)
     right_step(True, 0)
     right_send(True, 1)
-    mate_step(1)
     left_step("O", 0, 3)
     late(0, 2)
     pair_step(0)
     over_y(1)
+    left_step("Y", 1, 1)
     left_step("Y", 0, 3)
-    left_step("O", 1, 1)
+    left_step("O", 1, 2)
+    late(1, 1)
     left_step("O", 0, 4)
     late(0, 3)
     left_step("Y", 0, 4)
-    left_step("Y", 1, 1)
     late(0, 4)
+    left_step("Y", 1, 2)
+    over_y_on(1)
+    right_step(True, 1)
     right_step(False, 0)
-    over_y_on(1)
-    left_step("O", 1, 2)
+    left_step("O", 1, 3)
+    late(1, 2)
+    pair_step(1)
+    left_step("Y", 1, 3)
     right_rest(True, 0)
-    late(1, 1)
-    right_step(True, 1)
-    left_step("Y", 1, 2)
     right_rest(False, 0)
     shared(0)
     keep(0)
     triangle(0, 16)
-    left_step("O", 1, 3)
-    pair_step(1)
-    triangle(16, 24)
-    late(1, 2)
-    left_step("Y", 1, 3)
-    triangle(64, 16)
     left_step("O", 1, 4)
     late(1, 3)
+    triangle(16, 24)
     right_step(False, 1)
+    left_step("Y", 1, 4)
+    late(1, 4)
+    triangle(64, 16)
     triangle(80, 24)
     keep_triangle(0)
-    left_step("Y", 1, 4)
-    late(1, 4)
     right_rest(True, 1)
     right_rest(False, 1)
     shared(1)
@@ -473,19 +473,26 @@
     core, up, down, mate = me.at(e=1), me.at(z=1), me.at(z=-1), me.mate()
     east, west, north, south = me.at(x=1), me.at(x=-1), me.at(y=1), me.at(y=-1)
     gain = gain_ref[...]
-    loads = ([], [])
-
-    def load(g, src, dst):
-        made = pltpu.make_async_copy(src, dst, local.at[len(loads[0]) + len(loads[1])])
-        made.start()
-        loads[g].append(made)
+    loads = []
 
     for g in (0, 1):
-        for part in BACK.rows(g):
-            rows = pl.ds(part.start * 8, part.size * 8)
-            load(g, tri_hbm.at[:, rows], tri.at[:, rows])
-            load(g, rp_hbm.at[:, part], rp.at[:, part])
-            load(g, lp_hbm.at[:, :, part], lp.at[:, :, part])
+        start, size = BACK.whole(g)
+        for side in (1 - me.e, me.e):
+            part = pl.ds(pl.multiple_of(side * 64 + start, 8), size)
+            rows = pl.ds(pl.multiple_of((side * 64 + start) * 8, 64), size * 8)
+            for src, dst in (
+                (tri_hbm.at[:, rows], tri.at[:, rows]),
+                (rp_hbm.at[:, part], rp.at[:, part]),
+                (lp_hbm.at[:, :, part], lp.at[:, :, part]),
+            ):
+                made = pltpu.make_async_copy(src, dst, local.at[len(loads)])
+                made.start()
+                loads.append(made)
+
+    def loaded(count):
+        for made in loads[:count]:
+            made.wait()
+        del loads[:count]
 
     fill = Fill()
     left_w = jnp.concatenate([lg[...], lpw[...]], axis=1)
@@ -711,18 +718,17 @@
         for part in (low, high):
             add(column(1, 0), part.start, BACK.size[g], terms + [(pair_in, 0)], put_right)
 
-    for made in loads[0]:
-        made.wait()
+    loaded(3)
     panels_back(1 - me.e, 0, 24)
     met()
     core_send(0)
+    loaded(3)
     panels_back(me.e, 0, 24)
     right_first(0, 0)
     right_first(1, 0)
     left_step(0, 0, 0)
     left_step(1, 0, 0)
-    for made in loads[1]:
-        made.wait()
+    loaded(6)
     panels_back(1 - me.e, 24, 16)
     left_step(0, 0, 1)
     right_step(0, 0)
@@ -827,17 +833,9 @@
     )(*operands)
 
 
-def split_kernel(both, left_out, right_out, local):
-    made = []
-    for step in range(6):
-        src = both.at[pl.ds(step * 512, 512)]
-        out, shift = (left_out, 0) if step < 2 else (right_out, 2)
-        dst = out.at[pl.ds((step - shift) * 512, 512)]
-        made.append(pltpu.make_async_copy(src, dst, local.at[step]))
-    for one in made:
-        one.start()
-    for one in made:
-        one.wait()
+def split_kernel(both, left_out, right_out):
+    left_out[...] = both[:1024, :]
+    right_out[...] = both[1024:, :]
 
 
 def split(both):
@@ -847,9 +845,8 @@
             jax.ShapeDtypeStruct((1024, 128), BF),
             jax.ShapeDtypeStruct((2048, 128), BF),
         ),
-        in_specs=[ANY],
-        out_specs=(ANY, ANY),
-        scratch_shapes=[pltpu.SemaphoreType.DMA((6,))],
+        in_specs=[VMEM],
+        out_specs=(VMEM, VMEM),
         name="split_sides",
     )(both)
 

time: 168 us -> 144 us (0.86)
  Pallas kernels: 167 us -> 143 us
    pallas_call x1, Pallas kernels: 25 us -> 2.03 us  [split(): pl.pallas_call(split_kernel, out_shape=(jax.ShapeDtypeStruct((1024, 128),...]
where the time goes in v5:
time: 144 us; the launch traced here: 143 us
  Pallas kernels  143 us (99%)
    pallas_call x1, Pallas kernels, gather(): pl.pallas_call(gather_kernel, out_shape=(jax.ShapeDtypeStruct((2, 8, 128,...  63.5 us
    pallas_call x1, Pallas kernels, scatter(): pl.pallas_call(scatter_kernel, out_shape=jax.ShapeDtypeStruct((3072, 128)...  60.2 us
    pallas_call x1, Pallas kernels, middle(): pl.pallas_call(middle_kernel, grid=(64 // JS,), out_shape=(jax.ShapeDtype...  16.9 us

profile of v5, /device:TPU:1, one launch (start us, length us, event | category | flops | bytes accessed | tf_op | source)
XLA Modules:
  0.0 143.3 jit_solution(3082808563996925486)
XLA Ops:
  0.6 63.5 %gather_panels.1 = (bf16[2,8,128,16,128]{4,3,2,1,0:T(8,128)(2,1)}, bf16[8,128,16,128]{3,2,1,0:T(8,128)(2,1)}, f32[8,1024,128]{2,1,0:T(8,128)}) custom-call(bf16[1024,128]{1,0:T(8,128)(2,1)} %bitcast.10, bf16[2048,128]{1,0:T(8,128)(2,1)} %bitcast.8, s32[1,128]{1,0:T(1,128)} %bitcast.15, s32[1,64]{1,0:T(1,128)} %bitcast.17, s32[256]{0:T(256)} %mid_ref.3, ...), custom_call_target="tpu_custom_call" | custom-call | tf_op jit(solution)/shard_map/gather_panels/pallas_call | solution.py:433
  64.2 16.9 %middle.1 = (bf16[128,64,128]{2,1,0:T(8,128)(2,1)}, bf16[128,64,128]{2,1,0:T(8,128)(2,1)}, f32[8,1024,128]{2,1,0:T(8,128)}) custom-call(f32[8,1024,128]{2,1,0:T(8,128)} %get-tuple-element.12.tri_ref, bf16[128,64,128]{2,1,0:T(8,128)(2,1)} %tile_ref.1, bf16[128,64,128]{2,1,0:T(8,128)(2,1)} %up_ref.1, f32[1,128]{1,0:T(1,128)} %bitcast.13, ...), custom_call_target="tpu_custom_call" | custom-call | tf_op jit(solution)/shard_map/middle/pallas_call | solution.py:901
  81.0 60.2 %scatter_sums.1.both = bf16[3072,128]{1,0:T(8,128)(2,1)} custom-call(bf16[2,8,128,16,128]{4,3,2,1,0:T(8,128)(2,1)} %get-tuple-element.14.lp_hbm, bf16[8,128,16,128]{3,2,1,0:T(8,128)(2,1)} %get-tuple-element.15.rp_hbm, f32[8,1024,128]{2,1,0:T(8,128)} %get-tuple-element.16.tri_hbm, bf16[1024,128]{1,0:T(8,128)(2,1)} %bitcast.11, bf16[2048,128]{1,0:T(8,128)(2,1)} %bitcast.9, ...), custom_call_target="tpu_custom_call" | custom-call | tf_op jit(solution)/shard_map/scatter_sums/pallas_call | solution.py:798
  141.3 2.0 %split_sides.1 = (bf16[1024,128]{1,0:T(8,128)(2,1)}, bf16[2048,128]{1,0:T(8,128)(2,1)}) custom-call(bf16[3072,128]{1,0:T(8,128)(2,1)} %scatter_sums.1.both), custom_call_target="tpu_custom_call" | custom-call | tf_op jit(solution)/shard_map/split_sides/pallas_call | solution.py:842

commit v6 on v5

--- a/solution.py
+++ b/solution.py
@@ -858,39 +858,50 @@
     tri_ref, tile_ref, up_ref, in_gain_ref, gate_w_ref, mid_gain_ref, proj_w_ref,
     update_ref, d_tile_ref, d_tri_ref, flat, rstds,
 ):
-    mid_gain = jnp.broadcast_to(mid_gain_ref[...], (128, 128)).T
+    mid_gain = jnp.broadcast_to(mid_gain_ref[...], (256, 128)).T
     in_gain = in_gain_ref[...]
     proj_w = proj_w_ref[...]
     gate_w = gate_w_ref[...]
 
-    for j in range(JS):
-        normed, rstd = norm(tri_ref[0, pl.ds(j, 128, stride=8), :], 0)
-        d_tri_ref[0, pl.ds(j, 128, stride=8), :] = normed
-        rstds[pl.ds(j, 1), :] = rstd
+    def pair(j):
+        return pl.ds(j, 128, stride=8), pl.ds(j + 1, 128, stride=8)
+
+    for j in range(0, JS, 2):
+        one, two = pair(j)
+        both = jnp.concatenate([tri_ref[0, one, :], tri_ref[0, two, :]], axis=1)
+        normed, rstd = norm(both, 0)
+        d_tri_ref[0, one, :] = normed[:, :128]
+        d_tri_ref[0, two, :] = normed[:, 128:]
+        rstds[pl.ds(j // 2, 1), :] = rstd
         value = tn((normed * mid_gain).astype(BF), proj_w)
-        flat[pl.ds(j, 128, stride=8), :] = value
-
-    for t in range(8):
-        rows = pl.ds(t * 128, 128)
-        items = pl.ds(t * 16, 16)
-        tile = tile_ref[items].astype(F32).reshape(128, 128)
-        upstream = up_ref[items].astype(F32).reshape(128, 128)
+        flat[one, :] = value[:128]
+        flat[two, :] = value[128:]
+
+    for t in range(4):
+        rows = pl.ds(t * 256, 256)
+        items = pl.ds(t * 32, 32)
+        tile = tile_ref[items].astype(F32).reshape(256, 128)
+        upstream = up_ref[items].astype(F32).reshape(256, 128)
         normed, rstd = norm(tile, -1)
         gate = sigmoid(nn((normed * in_gain).astype(BF), gate_w))
         value = flat[rows, :]
-        update_ref[items] = (gate * value).reshape(16, 8, 128).astype(BF)
+        update_ref[items] = (gate * value).reshape(32, 8, 128).astype(BF)
         gated = upstream * gate
         flat[rows, :] = gated
         d_gate = (gated * value * (1.0 - gate)).astype(BF)
         d_norm = nt(d_gate, gate_w)
         d_tile = norm_back(normed, rstd, in_gain, d_norm, -1)
-        d_tile_ref[items] = d_tile.reshape(16, 8, 128).astype(BF)
-
-    for j in range(JS):
-        here = pl.ds(j, 128, stride=8)
-        normed, rstd = d_tri_ref[0, here, :], rstds[pl.ds(j, 1), :]
-        d_norm = nt(proj_w, flat[here, :].astype(BF))
-        d_tri_ref[0, here, :] = norm_back(normed, rstd, mid_gain, d_norm, 0)
+        d_tile_ref[items] = d_tile.reshape(32, 8, 128).astype(BF)
+
+    for j in range(0, JS, 2):
+        one, two = pair(j)
+        normed = jnp.concatenate([d_tri_ref[0, one, :], d_tri_ref[0, two, :]], axis=1)
+        gated = jnp.concatenate([flat[one, :], flat[two, :]], axis=0)
+        d_norm = nt(proj_w, gated.astype(BF))
+        rstd = rstds[pl.ds(j // 2, 1), :]
+        result = norm_back(normed, rstd, mid_gain, d_norm, 0)
+        d_tri_ref[0, one, :] = result[:, :128]
+        d_tri_ref[0, two, :] = result[:, 128:]
 
 
 def middle(tri, tile, upstream, in_gain, gate_w, mid_gain, proj_w):
@@ -908,7 +919,7 @@
         ),
         in_specs=[cube, cell, cell, line, whole, line, whole],
         out_specs=(cell, cell, cube),
-        scratch_shapes=[pltpu.VMEM((1024, 128), F32), pltpu.VMEM((JS, 128), F32)],
+        scratch_shapes=[pltpu.VMEM((1024, 128), F32), pltpu.VMEM((JS, 256), F32)],
         compiler_params=pltpu.CompilerParams(
             vmem_limit_bytes=LIMIT, dimension_semantics=("arbitrary",)
         ),

time: 144 us -> 141 us (0.979)
  Pallas kernels: 143 us -> 140 us
    pallas_call x1, Pallas kernels: 16.9 us -> 14.2 us  [middle(): pl.pallas_call(middle_kernel, grid=(64 // JS,), out_shape=(jax.ShapeDtype...]
where the time goes in v6:
time: 141 us
  Pallas kernels  140 us (99%)
    pallas_call x1, Pallas kernels, gather(): pl.pallas_call(gather_kernel, out_shape=(jax.ShapeDtypeStruct((2, 8, 128,...  63.5 us
    pallas_call x1, Pallas kernels, scatter(): pl.pallas_call(scatter_kernel, out_shape=jax.ShapeDtypeStruct((3072, 128)...  60.2 us
    pallas_call x1, Pallas kernels, middle(): pl.pallas_call(middle_kernel, grid=(64 // JS,), out_shape=(jax.ShapeDtype...  14.2 us

profile of v6, /device:TPU:1, one launch (start us, length us, event | category | flops | bytes accessed | tf_op | source)
XLA Modules:
  0.0 140.6 jit_solution(535904060090649350)
XLA Ops:
  0.6 63.5 %gather_panels.1 = (bf16[2,8,128,16,128]{4,3,2,1,0:T(8,128)(2,1)}, bf16[8,128,16,128]{3,2,1,0:T(8,128)(2,1)}, f32[8,1024,128]{2,1,0:T(8,128)}) custom-call(bf16[1024,128]{1,0:T(8,128)(2,1)} %bitcast.10, bf16[2048,128]{1,0:T(8,128)(2,1)} %bitcast.8, s32[1,128]{1,0:T(1,128)} %bitcast.15, s32[1,64]{1,0:T(1,128)} %bitcast.17, s32[256]{0:T(256)} %mid_ref.3, ...), custom_call_target="tpu_custom_call" | custom-call | tf_op jit(solution)/shard_map/gather_panels/pallas_call | solution.py:433
  64.2 14.2 %middle.1 = (bf16[128,64,128]{2,1,0:T(8,128)(2,1)}, bf16[128,64,128]{2,1,0:T(8,128)(2,1)}, f32[8,1024,128]{2,1,0:T(8,128)}) custom-call(f32[8,1024,128]{2,1,0:T(8,128)} %get-tuple-element.12.tri_ref, bf16[128,64,128]{2,1,0:T(8,128)(2,1)} %tile_ref.1, bf16[128,64,128]{2,1,0:T(8,128)(2,1)} %up_ref.1, f32[1,128]{1,0:T(1,128)} %bitcast.13, ...), custom_call_target="tpu_custom_call" | custom-call | tf_op jit(solution)/shard_map/middle/pallas_call | solution.py:912
  78.3 60.2 %scatter_sums.1.both = bf16[3072,128]{1,0:T(8,128)(2,1)} custom-call(bf16[2,8,128,16,128]{4,3,2,1,0:T(8,128)(2,1)} %get-tuple-element.14.lp_hbm, bf16[8,128,16,128]{3,2,1,0:T(8,128)(2,1)} %get-tuple-element.15.rp_hbm, f32[8,1024,128]{2,1,0:T(8,128)} %get-tuple-element.16.tri_hbm, bf16[1024,128]{1,0:T(8,128)(2,1)} %bitcast.11, bf16[2048,128]{1,0:T(8,128)(2,1)} %bitcast.9, ...), custom_call_target="tpu_custom_call" | custom-call | tf_op jit(solution)/shard_map/scatter_sums/pallas_call | solution.py:798
  138.6 2.0 %split_sides.1 = (bf16[1024,128]{1,0:T(8,128)(2,1)}, bf16[2048,128]{1,0:T(8,128)(2,1)}) custom-call(bf16[3072,128]{1,0:T(8,128)(2,1)} %scatter_sums.1.both), custom_call_target="tpu_custom_call" | custom-call | tf_op jit(solution)/shard_map/split_sides/pallas_call | solution.py:842
